TPU v7x, 256 devices: a whole 4x4x8 slice. The times are simulated.
256 devices in a mesh: section: 8 (over x, y_lo), expert: 16 (over z, core), dp: 2 (over y_hi).
Axes of the slice: x: 4, y: 4 (y_hi: 2, y_lo: 2; y = y_hi * 2 + y_lo), z: 8, core: 2. Of those that a mesh axis runs over, the one named last changes fastest.
Arguments:
- fwd_input: bfloat16 [8, 1536, 3584], P('section', ('expert', 'dp')), may hold values from -24 to 24
- back_saved: bfloat16 [2, 8, 1536, 3584], P(None, 'section', ('expert', 'dp')), may hold values from -24 to 24
- back_grad: bfloat16 [8, 1536, 3584], P('section', ('expert', 'dp')), may hold values from -6 to 6
- norm_gain: float32 [8, 3584], P('section'), may hold values from 0.3 to 3
- gate_weight: bfloat16 [8, 16, 3584, 1024], P('section', 'expert', 'dp'), may hold values from -0.09375 to 0.09375
- up_weight: bfloat16 [8, 16, 3584, 1024], P('section', 'expert', 'dp'), may hold values from -0.09375 to 0.09375
- down_weight: bfloat16 [8, 16, 1024, 3584], P('section', 'expert', None, 'dp'), may hold values from -0.1875 to 0.1875
- routes: int32 [4, 8, 1536, 2], P(None, 'section', ('expert', 'dp')), may hold values from 0 to 15, as said below
- slots: int32 [4, 8, 1536, 2], P(None, 'section', ('expert', 'dp')), may hold values from 0 to 6, as said below
- affinity: float32 [4, 8, 1536, 2], P(None, 'section', ('expert', 'dp')), may hold values from 0.05 to 1
Outputs:
- fwd_output: bfloat16 [8, 1536, 3584], P('section', ('expert', 'dp'))
- back_output: bfloat16 [8, 1536, 3584], P('section', ('expert', 'dp'))
Inputs may be any that keep to these rules, and one draw needn't show every extreme that they name: A token's routes name distinct experts. In each aligned block of 48 tokens of one index of the first dimension and one section, each expert is named at most 7 times, and one expert exactly 7 times; that expert is the same for all blocks of one index of the first dimension, one section and one dp index. Within one aligned block of 48 tokens, the routes to one expert hold distinct slots.
All inputs are finite; a program needn't handle non-finite values.
Results may differ from a plain program's by a relative error of at most 0.012.
Values may be sent and summed in bfloat16 or wider, within the bound.
No kernel may reach another device: no remote copies, remote signals or barrier semaphores. Data moves between devices by JAX's collectives and lax.ppermute only.
A program may use at most 128 MiB of HBM per device.

v0:
```python
import jax
import jax.numpy as jnp
from jax import lax
from jax.sharding import PartitionSpec as P

ROUTE_SCALE = 2.5
EPSILON = 1e-06


def from_behind(block, axis, distance):
    devices = range(lax.axis_size(axis))
    route = [(i - distance, i) for i in devices if i - distance in devices]
    return lax.ppermute(block, axis, route)


def normalize(inputs, gain):
    widened = inputs.astype(jnp.float32)
    inverse = lax.rsqrt(jnp.mean(widened * widened, axis=-1, keepdims=True) + EPSILON)
    return (widened, inverse, (widened * inverse * gain).astype(jnp.bfloat16))


def contract_last(left, right):
    return lax.dot_general(
        left, right, (((1,), (1,)), ((), ())), preferred_element_type=jnp.float32
    )


def expert_forward(rows, gate_w, up_w, down_w):
    gate = jnp.dot(rows, gate_w, preferred_element_type=jnp.float32)
    upper = jnp.dot(rows, up_w, preferred_element_type=jnp.float32)
    active = (gate * jax.nn.sigmoid(gate) * upper).astype(jnp.bfloat16)
    return jnp.dot(active, down_w, preferred_element_type=jnp.float32).astype(jnp.bfloat16)


def swiglu_backward(gate, upper, dactive):
    sigma = jax.nn.sigmoid(gate)
    dgate = (dactive * upper * sigma * (1.0 + gate * (1.0 - sigma))).astype(jnp.bfloat16)
    dupper = (dactive * gate * sigma).astype(jnp.bfloat16)
    return (dgate, dupper)


def expert_backward(rows, grads, gate_w, up_w, down_w):
    gate = jnp.dot(rows, gate_w, preferred_element_type=jnp.float32)
    upper = jnp.dot(rows, up_w, preferred_element_type=jnp.float32)
    dactive = contract_last(grads, down_w)
    dgate, dupper = swiglu_backward(gate, upper, dactive)
    return (contract_last(dgate, gate_w) + contract_last(dupper, up_w)).astype(jnp.bfloat16)


def body(
    fwd_input,
    back_saved,
    back_grad,
    norm_gain,
    gate_weight,
    up_weight,
    down_weight,
    routes,
    slots,
    affinity,
):
    experts = lax.axis_size("expert")
    tokens = fwd_input.shape[1]
    width = fwd_input.shape[2]
    topk = routes.shape[3]
    capacity = tokens * topk // experts + 1
    targets = routes[:, 0] * capacity + slots[:, 0]
    mixing = affinity[:, 0] / jnp.sum(affinity[:, 0], axis=-1, keepdims=True)
    gain = norm_gain[0]

    def place(values, target):
        placed = (
            jnp.zeros((experts * capacity, width), jnp.bfloat16)
            .at[target.reshape(-1)]
            .set(values.reshape(-1, width))
        )
        return placed.reshape(experts, capacity, width)

    gate_full, up_full, down_full = (
        lax.all_gather(gate_weight[0, 0], "dp", axis=0, tiled=True),
        lax.all_gather(up_weight[0, 0], "dp", axis=0, tiled=True),
        lax.all_gather(down_weight[0, 0], "dp", axis=1, tiled=True),
    )

    def run_forward(rows):
        return expert_forward(rows, gate_full, up_full, down_full)

    def run_backward(rows, grads):
        return expert_backward(rows, grads, gate_full, up_full, down_full)

    def section_slot(inputs, saved, grads, first, second):
        widened, inverse, normed = normalize(inputs, gain)
        forward_send = place(
            jnp.broadcast_to(normed[:, None, :], (tokens, topk, width)), targets[first]
        )
        saved_wide, saved_inverse, saved_normed = normalize(saved, gain)
        wide_grads = grads.astype(jnp.float32)
        sent = (ROUTE_SCALE * mixing[second][:, :, None] * wide_grads[:, None, :]).astype(
            jnp.bfloat16
        )
        backward_send = jnp.stack(
            [
                place(
                    jnp.broadcast_to(saved_normed[:, None, :], (tokens, topk, width)),
                    targets[second],
                ),
                place(sent, targets[second]),
            ]
        )
        arrived = lax.all_to_all(
            jnp.concatenate([forward_send[None], backward_send]),
            "expert",
            split_axis=1,
            concat_axis=1,
            tiled=True,
        )
        arrived = arrived.reshape(3, experts * capacity, width)
        results = jnp.stack(
            [run_forward(arrived[0]), run_backward(arrived[1], arrived[2])]
        ).reshape(2, experts, capacity, width)
        returned = lax.all_to_all(results, "expert", split_axis=1, concat_axis=1, tiled=True)
        forward_back = returned[0]
        backward_back = returned[1]
        picked = forward_back.reshape(-1, width)[targets[first]].astype(jnp.float32)
        outputs = (
            widened + ROUTE_SCALE * jnp.sum(mixing[first][:, :, None] * picked, axis=1)
        ).astype(jnp.bfloat16)
        dnormed = jnp.sum(
            backward_back.reshape(-1, width)[targets[second]].astype(jnp.float32), axis=1
        )
        weighted = dnormed * gain
        project = jnp.mean(weighted * saved_wide, axis=-1, keepdims=True)
        gradient = (
            wide_grads
            + saved_inverse * (weighted - saved_wide * saved_inverse * saved_inverse * project)
        ).astype(jnp.bfloat16)
        return (outputs, gradient)

    first_out, first_back = section_slot(fwd_input[0], back_saved[0, 0], back_grad[0], 0, 1)
    arrived_out = from_behind(first_out, "section", 1)
    arrived_back = from_behind(first_back, "section", -1)
    final_out, final_back = section_slot(arrived_out, back_saved[1, 0], arrived_back, 2, 3)
    return (final_out[None], final_back[None])


def solution(mesh):
    placed = (
        P("section", ("expert", "dp"), None),
        P(None, "section", ("expert", "dp"), None),
        P("section", ("expert", "dp"), None),
        P("section", None),
        P("section", "expert", "dp", None),
        P("section", "expert", "dp", None),
        P("section", "expert", None, "dp"),
        P(None, "section", ("expert", "dp"), None),
        P(None, "section", ("expert", "dp"), None),
        P(None, "section", ("expert", "dp"), None),
    )
    return jax.shard_map(
        body,
        mesh=mesh,
        in_specs=placed,
        out_specs=(P("section", ("expert", "dp"), None), P("section", ("expert", "dp"), None)),
        check_vma=False,
    )
```

profile of v0, /device:TPU:3, one launch (start us, length us, event | category | flops | bytes accessed | tf_op | source)
XLA Modules:
  0.0 631.1 jit_solution(6112946681624975535)
XLA Ops:
  12.9 1.8 scatter_custom_fusion.1
  15.0 1.3 broadcast_in_dim.12
  16.3 1.1 reshape.500
  17.4 2.3 scatter_custom_fusion
  19.8 1.2 broadcast_in_dim_reshape.6
  21.7 1.6 mul.314
  23.4 2.4 mul.315
  25.8 2.6 scatter_custom_fusion.2
  28.4 1.6 stack_reshape.13
  30.0 2.0 pad_maximum_fusion
  32.1 74.0 %all_to_all.20 = bf16[3,16,7,3584]{3,2,0,1:T(8,128)(2,1)S(1)} all-to-all(bf16[3,16,7,3584]{3,2,0,1:T(8,128)(2,1)S(1)} %copy.40), channel_id=1, replica_groups=mesh['section'=8,'expert'=16,'dp'=2] {'expert'}, dimensions={1} | all-to-all | bytes 4816896 | tf_op jit(solution)/shard_map/all_to_all | solution.py:110
  106.1 1.5 fusion.171
  107.6 1.5 squeeze.55
  109.0 2.3 squeeze.54
  111.7 4.3 fusion.28
  116.0 95.7 %all-gather.11.cloned.1.call-done = bf16[1,1,1024,3584]{3,2,1,0:T(8,128)(2,1)} async-done(((bf16[1,1,1024,1792]{3,2,1,0:T(8,128)(2,1)}), bf16[1,1,1024,3584]{3,2,1,0:T(8,128)(2,1)}) %all-gather.11.cloned.1.call-update) | async-done | bytes 7340048 | tf_op jit(solution)/shard_map/all_gather | solution.py:82
  211.6 5.7 fusion.4
  217.3 94.4 %all-gather.9.cloned.1.call-done = bf16[1,1,3584,1024]{3,2,1,0:T(8,128)(2,1)} async-done(((bf16[1,1,1792,1024]{3,2,1,0:T(8,128)(2,1)}), bf16[1,1,3584,1024]{3,2,1,0:T(8,128)(2,1)}) %all-gather.9.cloned.1.call-update) | async-done | bytes 7340048 | tf_op jit(solution)/shard_map/all_gather | solution.py:81
  311.7 6.7 %fusion.14 = f32[112,3584]{1,0:T(8,128)} fusion(bf16[1,1,3584,1024]{3,2,1,0:T(8,128)(2,1)} %all-gather.9.cloned.1.call-done, f32[112,1024]{1,0:T(8,128)S(1)} %fusion.4, f32[112,1024]{1,0:T(8,128)S(1)} %fusion.28), kind=kOutput, calls=%fused_computation.24 | convolution fusion | flops 822771712 | bytes 9863168 | tf_op jit(solution)/shard_map/dot_general | solution.py:23
  318.4 10.2 %fusion.41 = bf16[112,3584]{1,0:T(8,128)(2,1)} fusion(f32[112,3584]{1,0:T(8,128)} %fusion.14, bf16[1,1,3584,1024]{3,2,1,0:T(8,128)(2,1)} %all-gather.7.cloned.1.call-done, f32[112,1024]{1,0:T(8,128)S(1)} %fusion.4, bf16[112,3584]{1,0:T(8,128)(2,1)S(1)} %squeeze.55, bf16[1,1,3584,1024]{3,2,1,0:T(8,128)(2,1)} %all-gather.9.cloned.1.call-done, ...), kind=kOutput, calls=%fused_computation.45 | convolution fusion | flops 1646116864 | bytes 18808832 | tf_op jit(solution)/shard_map/dot_general | solution.py:23
  328.6 1.4 stack.19
  330.0 4.2 fusion.30
  334.2 8.4 %fusion.44 = bf16[112,3584]{1,0:T(8,128)(2,1)} fusion(bf16[1,1,1024,3584]{3,2,1,0:T(8,128)(2,1)} %all-gather.11.cloned.1.call-done, bf16[112,3584]{1,0:T(8,128)(2,1)S(1)} %squeeze.50, bf16[1,1,3584,1024]{3,2,1,0:T(8,128)(2,1)} %all-gather.9.cloned.1.call-done, f32[112,1024]{1,0:T(8,128)S(1)} %fusion.30), kind=kOutput, calls=%fused_computation.46 | convolution fusion | flops 1645256704 | bytes 16744448 | tf_op jit(solution)/shard_map/dot_general | solution.py:32
  342.6 1.4 stack.18
  344.5 3.4 copy.41
  347.9 7.7 %all-to-all-start.1 = ((bf16[2,16,7,3584]{3,0,2,1:T(2,128)(2,1)}), bf16[2,16,7,3584]{3,0,2,1:T(2,128)(2,1)S(1)}, u32[]{:S(2)}, u32[]{:S(2)}) async-start(bf16[2,16,7,3584]{3,0,2,1:T(2,128)(2,1)} %copy.41), calls=%async_computation.1 | async-start | bytes 3211264 | tf_op jit(solution)/shard_map/all_to_all | solution.py:121
  360.8 33.9 %all-to-all-done.1 = bf16[2,16,7,3584]{3,0,2,1:T(2,128)(2,1)S(1)} async-done(((bf16[2,16,7,3584]{3,0,2,1:T(2,128)(2,1)}), bf16[2,16,7,3584]{3,0,2,1:T(2,128)(2,1)S(1)}, u32[]{:S(2)}, u32[]{:S(2)}) %all-to-all-start.1) | async-done | bytes 1605664 | tf_op jit(solution)/shard_map/all_to_all | solution.py:121
  394.7 7.9 %slice_reduce_fusion.3 = (bf16[16,7,3584]{2,1,0:T(8,128)(2,1)}, bf16[16,7,3584]{2,1,0:T(8,128)(2,1)S(1)}) fusion(bf16[2,16,7,3584]{3,0,2,1:T(2,128)(2,1)S(1)} %all-to-all-done.1), kind=kLoop, calls=%fused_computation.55 | loop fusion | bytes 3211264 | tf_op jit(solution)/shard_map/slice | solution.py:122
  402.5 1.5 reshape_squeeze.28
  404.0 2.1 gather_fusion
  406.1 2.0 reshape.551
  408.2 1.9 multiply_reduce_fusion.1
  410.9 2.4 collective-permute-start
  414.6 2.0 reshape.552
  416.6 3.0 reduce_sum.105
  419.9 4.1 collective-permute-done
  424.6 1.9 collective-permute-start.1
  427.2 1.8 scatter_custom_fusion.3
  429.0 1.2 broadcast_in_dim_reshape.7
  430.8 1.8 scatter_custom_fusion.4
  432.6 1.2 stack_reshape.14
  433.8 1.9 collective-permute-done.1
  437.4 2.5 scatter_custom_fusion.5
  439.9 1.4 stack_reshape.15
  442.2 69.3 %all_to_all.21 = bf16[3,16,7,3584]{3,2,0,1:T(8,128)(2,1)S(1)} all-to-all(bf16[3,16,7,3584]{3,2,0,1:T(8,128)(2,1)S(1)} %copy.48), channel_id=1, replica_groups=mesh['section'=8,'expert'=16,'dp'=2] {'expert'}, dimensions={1} | all-to-all | bytes 4816896 | tf_op jit(solution)/shard_map/all_to_all | solution.py:110
  511.5 1.4 fusion.170
  513.3 4.3 fusion.24
  517.5 7.5 %fusion.47 = bf16[112,3584]{1,0:T(8,128)(2,1)S(1)} fusion(bf16[1,1,1024,3584]{3,2,1,0:T(8,128)(2,1)} %all-gather.11.cloned.1.call-done, bf16[112,3584]{1,0:T(8,128)(2,1)S(1)} %squeeze.58, bf16[1,1,3584,1024]{3,2,1,0:T(8,128)(2,1)} %all-gather.9.cloned.1.call-done, f32[112,1024]{1,0:T(8,128)S(1)} %fusion.24), kind=kOutput, calls=%fused_computation.47 | convolution fusion | flops 1645256704 | bytes 16744448 | tf_op jit(solution)/shard_map/dot_general | solution.py:32
  525.0 1.2 stack.21
  526.3 2.6 squeeze.60
  528.8 2.3 squeeze.59
  531.2 4.7 fusion.22
  535.9 5.6 fusion
  542.3 3.7 fusion.8
  545.9 9.8 %fusion.38 = bf16[112,3584]{1,0:T(8,128)(2,1)S(1)} fusion(f32[112,3584]{1,0:T(8,128)} %fusion.8, bf16[1,1,3584,1024]{3,2,1,0:T(8,128)(2,1)} %all-gather.7.cloned.1.call-done, f32[112,1024]{1,0:T(8,128)} %copy-done.3, bf16[112,3584]{1,0:T(8,128)(2,1)} %squeeze.60, bf16[1,1,3584,1024]{3,2,1,0:T(8,128)(2,1)} %all-gather.9.cloned.1.call-done, ...), kind=kOutput, calls=%fused_computation.44 | convolution fusion | flops 1646116864 | bytes 18808832 | tf_op jit(solution)/shard_map/dot_general | solution.py:23
  556.5 3.1 copy.49
  559.6 3.6 all-to-all-start.3
  565.0 37.1 %all-to-all-done.3 = bf16[2,16,7,3584]{3,0,2,1:T(2,128)(2,1)S(1)} async-done(((bf16[2,16,7,3584]{3,0,2,1:T(2,128)(2,1)}), bf16[2,16,7,3584]{3,0,2,1:T(2,128)(2,1)S(1)}, u32[]{:S(2)}, u32[]{:S(2)}) %all-to-all-start.3) | async-done | bytes 1605664 | tf_op jit(solution)/shard_map/all_to_all | solution.py:121
  602.1 7.6 %slice_reduce_fusion = (bf16[16,7,3584]{2,1,0:T(8,128)(2,1)S(1)}, bf16[16,7,3584]{2,1,0:T(8,128)(2,1)}) fusion(bf16[2,16,7,3584]{3,0,2,1:T(2,128)(2,1)S(1)} %all-to-all-done.3), kind=kLoop, calls=%fused_computation.52 | loop fusion | bytes 3211264 | tf_op jit(solution)/shard_map/slice | solution.py:123
  611.9 1.6 reduce_sum.108
  614.2 1.5 reshape_squeeze.32
  615.7 1.8 gather_fusion.2
  617.6 2.3 reshape.553
  619.8 2.7 multiply_reduce_fusion
  (173 shorter events, 27.6 us)
Async XLA Ops:
  7.2 104.5 %all-gather.7.cloned.1.call-start = ((), (), s32[]{:S(2)}) async-start(), calls=%async_computation.4 | async-start | bytes 11010048 | tf_op jit(solution)/shard_map/all_gather | solution.py:80
  7.9 203.7 %all-gather.11.cloned.1.call-start = ((), (), s32[]{:S(2)}) async-start(), calls=%async_computation.6 | async-start | bytes 11010048 | tf_op jit(solution)/shard_map/all_gather | solution.py:82
  8.6 1.0 copy-start.8
  8.7 1.2 copy-start
  8.7 1.4 copy-start.28
  8.7 1.4 copy-start.29
  8.7 2.4 copy-start.24
  8.7 2.5 copy-start.13
  8.7 2.5 copy-start.25
  8.7 303.0 %all-gather.9.cloned.1.call-start = ((), (), s32[]{:S(2)}) async-start(), calls=%async_computation.5 | async-start | bytes 11010048 | tf_op jit(solution)/shard_map/all_gather | solution.py:81
  10.1 0.6 copy-start.22
  11.3 3.7 copy-start.15
  11.3 3.6 copy-start.26
  344.4 11.1 %copy-start.23 = (s32[4,1,48,2]{2,3,1,0:T(2,128)S(1)}, s32[4,1,48,2]{2,3,1,0:T(2,128)}, u32[]{:S(2)}) copy-start(s32[4,1,48,2]{2,3,1,0:T(2,128)} %copy-done.22) | copy-start | bytes 4612
  344.5 11.9 %copy-start.36 = (f32[48,2]{0,1:T(2,128)S(1)}, f32[48,2]{0,1:T(2,128)}, u32[]{:S(2)}) copy-start(f32[48,2]{0,1:T(2,128)} %get-tuple-element.26) | copy-start | bytes 1156
  344.5 12.8 %copy-start.34 = (s32[1,1,48,2]{2,3,1,0:T(2,128)S(1)}, s32[1,1,48,2]{2,3,1,0:T(2,128)}, u32[]{:S(2)}) copy-start(s32[1,1,48,2]{2,3,1,0:T(2,128)} %get-tuple-element.28) | copy-start | bytes 1156
  344.5 13.6 %copy-start.35 = (f32[1,48,2]{1,2,0:T(2,128)S(1)}, f32[1,48,2]{1,2,0:T(2,128)}, u32[]{:S(2)}) copy-start(f32[1,48,2]{1,2,0:T(2,128)} %get-tuple-element.24) | copy-start | bytes 1156
  344.5 14.4 %copy-start.33 = (s32[1,1,48,2]{2,3,1,0:T(2,128)S(1)}, s32[1,1,48,2]{2,3,1,0:T(2,128)}, u32[]{:S(2)}) copy-start(s32[1,1,48,2]{2,3,1,0:T(2,128)} %get-tuple-element.27) | copy-start | bytes 1156
  347.9 46.8 %all-to-all-start.1 = ((bf16[2,16,7,3584]{3,0,2,1:T(2,128)(2,1)}), bf16[2,16,7,3584]{3,0,2,1:T(2,128)(2,1)S(1)}, u32[]{:S(2)}, u32[]{:S(2)}) async-start(bf16[2,16,7,3584]{3,0,2,1:T(2,128)(2,1)} %copy.41), calls=%async_computation.1 | async-start | bytes 3211264 | tf_op jit(solution)/shard_map/all_to_all | solution.py:121
  404.0 4.2 copy-start.21
  408.2 5.4 copy-start.19
  410.9 13.0 %collective-permute-start = (bf16[48,3584]{1,0:T(8,128)(2,1)}, bf16[48,3584]{1,0:T(8,128)(2,1)S(1)}, u32[]{:S(2)}, u32[]{:S(2)}) collective-permute-start(bf16[48,3584]{1,0:T(8,128)(2,1)} %fusion.109), channel_id=1, source_target_pairs={{0,32},{32,64},{64,96},{96,128},{128,160},{160,192},{192,224},{1,3... | collective-permute-start | bytes 1032200 | tf_op jit(solution)/shard_map/ppermute | solution.py:13
  414.5 5.0 copy-start.16
  414.6 9.6 %copy-start.14 = (bf16[1,48,3584]{2,1,0:T(8,128)(2,1)S(1)}, bf16[1,48,3584]{2,1,0:T(8,128)(2,1)}, u32[]{:S(2)}) copy-start(bf16[1,48,3584]{2,1,0:T(8,128)(2,1)} %param.12) | copy-start | bytes 1032196
  414.6 9.6 %copy-start.27 = (f32[48]{0:T(128)S(1)}, f32[48]{0:T(128)}, u32[]{:S(2)}) copy-start(f32[48]{0:T(128)} %copy-done.26) | copy-start | bytes 580
  419.6 7.0 %copy-start.41 = (s32[96,1]{0,1:T(1,128)S(1)}, s32[96,1]{0,1:T(1,128)}, u32[]{:S(2)}) copy-start(s32[96,1]{0,1:T(1,128)} %reshape_squeeze.30) | copy-start | bytes 1156
  419.6 7.0 %copy-start.42 = (s32[96,1]{0,1:T(1,128)S(1)}, s32[96,1]{0,1:T(1,128)}, u32[]{:S(2)}) copy-start(s32[96,1]{0,1:T(1,128)} %reshape_squeeze.29) | copy-start | bytes 1156
  419.9 7.1 %copy-start.37 = (f32[48]{0:T(128)}, f32[48]{0:T(128)S(1)}, u32[]{:S(2)}) copy-start(f32[48]{0:T(128)S(1)} %add_rsqrt_fusion) | copy-start | bytes 580
  423.9 3.3 copy-start.9
  424.6 11.1 %collective-permute-start.1 = (bf16[48,3584]{1,0:T(8,128)(2,1)S(1)}, bf16[48,3584]{1,0:T(8,128)(2,1)S(1)}, u32[]{:S(2)}, u32[]{:S(2)}) collective-permute-start(bf16[48,3584]{1,0:T(8,128)(2,1)S(1)} %get-tuple-element.15), channel_id=1, source_target_pairs={{32,0},{64,32},{96,64},{128,96},{160,128},{192,160},{224,192},{33,... | collective-permute-start | bytes 1032200 | tf_op jit(solution)/shard_map/ppermute | solution.py:13
  432.6 4.8 copy-start.39
  435.7 0.7 copy-start.11
  437.4 4.0 copy-start.5
  437.4 4.0 copy-start.6
  526.3 16.0 %slice-start = ((s8[7340032]{0:T(1024)(128)(4,1)}), s8[3145728]{0:T(1024)(128)(4,1)S(1)}, s32[]{:S(2)}) async-start(s8[7340032]{0:T(1024)(128)(4,1)} %bitcast.165), calls=%async_computation.7 | async-start | bytes 6291456
  531.2 4.7 copy-start.7
  531.2 11.1 %slice-start.1 = ((s8[7340032]{0:T(1024)(128)(4,1)}), s8[4194304]{0:T(1024)(128)(4,1)S(1)}, s32[]{:S(2)}) async-start(s8[7340032]{0:T(1024)(128)(4,1)} %bitcast.165), calls=%async_computation.8 | async-start | bytes 8388608
  535.8 5.6 copy-start.2
  541.5 0.8 copy-start.3
  545.9 10.1 %copy-start.4 = (bf16[1,16,7,3584]{3,2,1,0:T(8,128)(2,1)S(1)}, bf16[1,16,7,3584]{3,2,1,0:T(8,128)(2,1)}, u32[]{:S(2)}) copy-start(bf16[1,16,7,3584]{3,2,1,0:T(8,128)(2,1)} %stack.21) | copy-start | bytes 2408452
  556.5 6.8 %copy-start.32 = (s32[48,2,1]{0,1,2:T(2,128)S(1)}, s32[48,2,1]{0,1,2:T(2,128)}, u32[]{:S(2)}) copy-start(s32[48,2,1]{0,1,2:T(2,128)} %get-tuple-element.19) | copy-start | bytes 1156
  556.5 7.0 %copy-start.31 = (s32[48,2,1]{0,1,2:T(2,128)S(1)}, s32[48,2,1]{0,1,2:T(2,128)}, u32[]{:S(2)}) copy-start(s32[48,2,1]{0,1,2:T(2,128)} %get-tuple-element.22) | copy-start | bytes 1156
  556.5 7.2 %copy-start.30 = (f32[48,2]{0,1:T(2,128)S(1)}, f32[48,2]{0,1:T(2,128)}, u32[]{:S(2)}) copy-start(f32[48,2]{0,1:T(2,128)} %get-tuple-element.23) | copy-start | bytes 1156
  559.6 42.4 %all-to-all-start.3 = ((bf16[2,16,7,3584]{3,0,2,1:T(2,128)(2,1)}), bf16[2,16,7,3584]{3,0,2,1:T(2,128)(2,1)S(1)}, u32[]{:S(2)}, u32[]{:S(2)}) async-start(bf16[2,16,7,3584]{3,0,2,1:T(2,128)(2,1)} %copy.49), calls=%async_computation.3 | async-start | bytes 3211264 | tf_op jit(solution)/shard_map/all_to_all | solution.py:121
  611.0 2.5 copy-start.1
  611.0 2.5 copy-start.17
  613.5 2.2 copy-start.20
  617.5 5.0 copy-start.12
  617.5 5.0 copy-start.18
  617.5 5.0 copy-start.38
  617.5 5.0 copy-start.40
  617.5 6.0 copy-start.10
Sparse Core Ops, SparseCore 0:
  9.8 101.7 all-gather.6
  113.4 98.2 all-gather.10
  213.4 98.2 all-gather.8
where the time goes:
time: 640 us; the launch traced here: 631 us
  waiting for transfers between devices  269 us (42%)
  blocking collectives  143 us (22%)
  local copies, waits for them, and re-layouts  86.7 us (14%)
  matrix products  75 us (12%)
  other arithmetic  26.4 us (4%)
  starting transfers between devices  15.7 us (2%)
  between operations  15 us (2%)
    all_to_all x2, blocking collectives, section_slot(): lax.all_to_all(jnp.concatenate([forward_send[None], backward_send]), 'exp...  143 us
    all_gather x1, waiting for transfers between devices, body(): lax.all_gather(down_weight[0, 0], 'dp', axis=1, tiled=True)  95.7 us
    all_gather x1, waiting for transfers between devices, body(): lax.all_gather(up_weight[0, 0], 'dp', axis=0, tiled=True)  94.4 us
    all_to_all x2, waiting for transfers between devices, section_slot(): lax.all_to_all(results, 'expert', split_axis=1, concat_axis=1, tiled=True)  70.9 us
    dot_general x6, matrix products, contract_last(): lax.dot_general(left, right, (((1,), (1,)), ((), ())), preferred_element_...  41.7 us
    dot_general x2, matrix products, expert_forward(): jnp.dot(active, down_w, preferred_element_type=jnp.float32)  15.9 us
  transfers between devices with their start and end apart: 7, of which 6 were waited for; matrix products, arithmetic and copies ran while one was open for 9% of the time, Pallas kernels for 0%

commit v1 on v0

v1 whole, which is shorter than its diff:
```python
import jax
import jax.numpy as jnp
from jax import lax
from jax.sharding import PartitionSpec as P

ROUTE_SCALE = 2.5
EPSILON = 1e-06
GROUP = 16
BF16 = jnp.bfloat16
F32 = jnp.float32


def swap_dp(value):
    return lax.ppermute(value, "dp", [(0, 1), (1, 0)])


def move_section(value, step, flip_dp=False):
    sections = lax.axis_size("section")
    halves = lax.axis_size("dp")
    route = []
    for s in range(sections):
        if 0 <= s + step < sections:
            for d in range(halves):
                to = 1 - d if flip_dp else d
                route.append((s * halves + d, (s + step) * halves + to))
    return lax.ppermute(value, ("section", "dp"), route)


def to_experts(rows):
    groups = rows.reshape(-1, GROUP, rows.shape[-1])
    moved = lax.all_to_all(groups, "expert", split_axis=0, concat_axis=0, tiled=True)
    return moved.reshape(rows.shape)


def contract_last(left, right):
    return lax.dot_general(left, right, (((1,), (1,)), ((), ())), preferred_element_type=F32)


def matmul(left, right):
    return jnp.dot(left, right, preferred_element_type=F32)


def pick(selector, rows):
    return lax.dot_general(selector, rows, (((0,), (0,)), ((), ())), preferred_element_type=F32)


def body(
    fwd_input,
    back_saved,
    back_grad,
    norm_gain,
    gate_weight,
    up_weight,
    down_weight,
    routes,
    slots,
    affinity,
):
    experts = lax.axis_size("expert")
    tokens = fwd_input.shape[1]
    width = fwd_input.shape[2]
    half = width // 2
    capacity = 7
    row_count = experts * GROUP
    side = lax.axis_index("dp")
    gate_w, up_w, down_w = gate_weight[0, 0], up_weight[0, 0], down_weight[0, 0]
    gain = norm_gain[0]
    gain_half = lax.dynamic_slice(gain, (side * half,), (half,))

    x0, s0, s1, g0 = fwd_input[0], back_saved[0, 0], back_saved[1, 0], back_grad[0]

    def inverse_of(value):
        wide = value.astype(F32)
        return lax.rsqrt(jnp.mean(wide * wide, axis=-1) + EPSILON)

    targets = routes[:, 0] * GROUP + slots[:, 0] + side * capacity
    mixing = affinity[:, 0] / jnp.sum(affinity[:, 0], axis=-1, keepdims=True)
    scalars = jnp.concatenate(
        [
            jnp.stack([inverse_of(x0), inverse_of(s0), inverse_of(s1)]),
            jnp.transpose(targets.astype(F32), (0, 2, 1)).reshape(8, tokens),
            jnp.transpose(mixing, (0, 2, 1)).reshape(8, tokens),
        ]
    )

    def in_order(own, other):
        first = jnp.where(side == 0, own, other)
        second = jnp.where(side == 0, other, own)
        return first, second

    first, second = in_order(scalars, swap_dp(scalars))
    table = jnp.concatenate([first, second], axis=1)
    inverses = table[:3]
    marks = table[3:11].astype(jnp.int32).reshape(4, 2, -1)
    mixes = table[11:].reshape(4, 2, -1)

    def exchange_halves(value):
        lead = value.shape[:-1]
        own = lax.dynamic_slice_in_dim(value, side * half, half, axis=-1)
        other = lax.dynamic_slice_in_dim(value, (1 - side) * half, half, axis=-1)
        a, b = in_order(own, swap_dp(other))
        return jnp.concatenate([a, b], axis=-2)

    def selectors(index):
        rows = lax.broadcasted_iota(jnp.int32, (row_count, 2 * tokens), 0)
        return [(rows == marks[index, k][None, :]).astype(BF16) for k in range(2)]

    def normed_of(value, inverse):
        return (value.astype(F32) * inverse[:, None] * gain_half).astype(BF16)

    def place_same(index, value):
        a, b = selectors(index)
        return matmul(a + b, value).astype(BF16)

    def place_pair(index, pair):
        a, b = selectors(index)
        return matmul(
            jnp.concatenate([a, b], axis=1), jnp.concatenate(pair, axis=0)
        ).astype(BF16)

    def dp_sum(parts):
        sent = jnp.concatenate([part.astype(BF16) for part in parts], axis=1)
        got = swap_dp(sent).astype(F32)
        hidden = parts[0].shape[1]
        return [p + got[:, i * hidden : (i + 1) * hidden] for i, p in enumerate(parts)]

    def gate_up_parts(rows):
        return [matmul(rows, gate_w), matmul(rows, up_w)]

    def expert_forward(rows):
        gate, upper = dp_sum(gate_up_parts(rows))
        active = (gate * jax.nn.sigmoid(gate) * upper).astype(BF16)
        return matmul(active, down_w).astype(BF16)

    def expert_backward(gate, upper, dactive):
        sigma = jax.nn.sigmoid(gate)
        dgate = (dactive * upper * sigma * (1.0 + gate * (1.0 - sigma))).astype(BF16)
        dupper = (dactive * gate * sigma).astype(BF16)
        return (contract_last(dgate, gate_w) + contract_last(dupper, up_w)).astype(BF16)

    def combine_forward(index, value, rows):
        a, b = selectors(index)
        m = mixes[index]
        total = m[0][:, None] * pick(a, rows) + m[1][:, None] * pick(b, rows)
        return (value.astype(F32) + ROUTE_SCALE * total).astype(BF16)

    def sent_pair(index, grads):
        wide = grads.astype(F32)
        return [
            (ROUTE_SCALE * mixes[index, k][:, None] * wide).astype(BF16) for k in range(2)
        ]

    def combine_backward(index, saved, inverse, grads, rows):
        a, b = selectors(index)
        dnormed = pick(a, rows) + pick(b, rows)
        weighted = dnormed * gain_half
        wide = saved.astype(F32)
        part = jnp.sum(weighted * wide, axis=-1)[None]
        project = ((part + swap_dp(part)) / width)[0][:, None]
        inv = inverse[:, None]
        return (
            grads.astype(F32) + inv * (weighted - wide * inv * inv * project)
        ).astype(BF16)

    x0h = exchange_halves(x0)
    x0_rows = to_experts(place_same(0, normed_of(x0h, inverses[0])))
    sg = exchange_halves(jnp.stack([s0, g0]))
    s0h, g0h = sg[0], sg[1]
    s0_rows = to_experts(place_same(1, normed_of(s0h, inverses[1])))
    g0_rows = to_experts(place_pair(1, sent_pair(1, g0h)))
    out0 = expert_forward(x0_rows)
    s1h = exchange_halves(s1)
    s1_rows = to_experts(place_same(3, normed_of(s1h, inverses[2])))
    gate0, upper0, dactive0 = dp_sum(gate_up_parts(s0_rows) + [contract_last(g0_rows, down_w)])
    dexp0 = expert_backward(gate0, upper0, dactive0)
    gate1, upper1 = dp_sum(gate_up_parts(s1_rows))

    first_out = combine_forward(0, x0h, to_experts(out0))
    wide_out = first_out.astype(F32)
    square = jnp.sum(wide_out * wide_out, axis=-1)[None]
    x2h = move_section(first_out, 1)
    square_own = move_section(square, 1)
    square_other = move_section(square, 1, flip_dp=True)
    inverse2 = lax.rsqrt((square_own + square_other)[0] / width + EPSILON)
    x2_rows = to_experts(place_same(2, normed_of(x2h, inverse2)))

    first_back = combine_backward(1, s0h, inverses[1], g0h, to_experts(dexp0))
    g3h = move_section(first_back, -1)
    g3_rows = to_experts(place_pair(3, sent_pair(3, g3h)))

    out2 = expert_forward(x2_rows)
    final_out = combine_forward(2, x2h, to_experts(out2))
    (dactive1,) = dp_sum([contract_last(g3_rows, down_w)])
    dexp1 = expert_backward(gate1, upper1, dactive1)
    final_back = combine_backward(3, s1h, inverses[2], g3h, to_experts(dexp1))

    def restore(value):
        first, second = value[:tokens], value[tokens:]
        mine = jnp.where(side == 0, first, second)
        theirs = jnp.where(side == 0, second, first)
        a, b = in_order(mine, swap_dp(theirs))
        return jnp.concatenate([a, b], axis=-1)

    return (restore(final_out)[None], restore(final_back)[None])


def solution(mesh):
    placed = (
        P("section", ("expert", "dp"), None),
        P(None, "section", ("expert", "dp"), None),
        P("section", ("expert", "dp"), None),
        P("section", None),
        P("section", "expert", "dp", None),
        P("section", "expert", "dp", None),
        P("section", "expert", None, "dp"),
        P(None, "section", ("expert", "dp"), None),
        P(None, "section", ("expert", "dp"), None),
        P(None, "section", ("expert", "dp"), None),
    )
    return jax.shard_map(
        body,
        mesh=mesh,
        in_specs=placed,
        out_specs=(P("section", ("expert", "dp"), None), P("section", ("expert", "dp"), None)),
        check_vma=False,
    )
```

time: 640 us -> 381 us (0.60); the launches traced: 631 us -> 379 us
  blocking collectives: 143 us -> 0 us
  local copies, waits for them, and re-layouts: 86.7 us -> 2.82 us
  starting transfers between devices: 15.7 us -> 86.5 us
  waiting for transfers between devices: 269 us -> 206 us
  between operations: 15 us -> 1.33 us
  matrix products: 75 us -> 63.2 us
  other arithmetic: 26.4 us -> 19.1 us
    all_gather x3 -> x0, waiting for transfers between devices: 190 us -> none  [the longest x1 95.7 us: body(): lax.all_gather(down_weight[0, 0], 'dp', axis=1, tiled=True)]
    all_to_all x2 -> x0, blocking collectives: 143 us -> none  [section_slot(): lax.all_to_all(jnp.concatenate([forward_send[None], backward_send]), 'exp...]
    ppermute x2 -> x17, waiting for transfers between devices: 5.93 us -> 100 us  [the longest x13 84.1 us: swap_dp(): return lax.ppermute(value, 'dp', [(0, 1), (1, 0)])]
    all_to_all x2 -> x10, starting transfers between devices: 11.3 us -> 59.5 us  [to_experts(): lax.all_to_all(groups, 'expert', split_axis=0, concat_axis=0, tiled=True)]
    all_to_all x2 -> x10, waiting for transfers between devices: 70.9 us -> 105 us  [to_experts(): lax.all_to_all(groups, 'expert', split_axis=0, concat_axis=0, tiled=True)]
    ppermute x2 -> x17, starting transfers between devices: 4.31 us -> 27 us  [the longest x13 16.5 us: swap_dp(): return lax.ppermute(value, 'dp', [(0, 1), (1, 0)])]
    another operation x20 -> x0, local copies, waits for them, and re-layouts: 22.7 us -> none  [the longest x6 10.8 us: section_slot(): jnp.stack([run_forward(arrived[0]), run_backward(arrived[1], arrived[2])])]
    dot_general x6, matrix products: 41.7 us -> 21.6 us  [contract_last(): lax.dot_general(left, right, (((1,), (1,)), ((), ())), preferred_element_...]
  transfers between devices with their start and end apart: 7 -> 27, of which waited for: 6 -> 21; matrix products, arithmetic and copies ran while one was open for 9% -> 20% of each run, Pallas kernels for 0% -> 0%
where the time goes in v1:
time: 381 us; the launch traced here: 379 us
  waiting for transfers between devices  206 us (54%)
  starting transfers between devices  86.5 us (23%)
  matrix products  63.2 us (17%)
  other arithmetic  19.1 us (5%)
    all_to_all x10, waiting for transfers between devices, to_experts(): lax.all_to_all(groups, 'expert', split_axis=0, concat_axis=0, tiled=True)  105 us
    ppermute x13, waiting for transfers between devices, swap_dp(): return lax.ppermute(value, 'dp', [(0, 1), (1, 0)])  84.1 us
    all_to_all x10, starting transfers between devices, to_experts(): lax.all_to_all(groups, 'expert', split_axis=0, concat_axis=0, tiled=True)  59.5 us
    dot_general x16, matrix products, matmul(): return jnp.dot(left, right, preferred_element_type=F32)  38.6 us
    dot_general x6, matrix products, contract_last(): lax.dot_general(left, right, (((1,), (1,)), ((), ())), preferred_element_...  21.6 us
    ppermute x13, starting transfers between devices, swap_dp(): return lax.ppermute(value, 'dp', [(0, 1), (1, 0)])  16.5 us
    ppermute x4, waiting for transfers between devices, move_section(): return lax.ppermute(value, ('section', 'dp'), route)  16.3 us
    ppermute x4, starting transfers between devices, move_section(): return lax.ppermute(value, ('section', 'dp'), route)  10.6 us
  transfers between devices with their start and end apart: 27, of which 21 were waited for; matrix products, arithmetic and copies ran while one was open for 20% of the time, Pallas kernels for 0%

profile of v1, /device:TPU:3, one launch (start us, length us, event | category | flops | bytes accessed | tf_op | source)
XLA Modules:
  0.0 378.6 jit_solution(16816842508566710513)
XLA Ops:
  5.6 3.0 collective-permute-start.1
  11.1 5.0 %collective-permute-done = bf16[48,1792]{1,0:T(8,128)(2,1)S(1)} collective-permute-done((bf16[48,1792]{1,0:T(8,128)(2,1)S(1)}, bf16[48,1792]{1,0:T(8,128)(2,1)S(1)}, u32[]{:S(2)}, u32[]{:S(2)}) %collective-permute-start) | collective-permute-done | bytes 172064 | tf_op jit(solution)/shard_map/ppermute | solution.py:14
  17.0 1.4 convolution_convert_fusion.3
  18.5 10.3 %all-to-all-start = ((bf16[16,16,1792]{2,1,0:T(8,128)(2,1)}), bf16[16,16,1792]{2,1,0:T(8,128)(2,1)S(1)}, u32[]{:S(2)}, u32[]{:S(2)}) async-start(bf16[16,16,1792]{2,1,0:T(8,128)(2,1)} %bitcast.16), calls=%async_computation | async-start | bytes 1835008 | tf_op jit(solution)/shard_map/all_to_all | solution.py:31
  29.9 10.9 %collective-permute-done.8 = bf16[2,48,1792]{2,1,0:T(8,128)(2,1)S(1)} collective-permute-done((bf16[2,48,1792]{2,1,0:T(8,128)(2,1)S(1)}, bf16[2,48,1792]{2,1,0:T(8,128)(2,1)S(1)}, u32[]{:S(2)}, u32[]{:S(2)}) %collective-permute-start.8) | collective-permute-done | bytes 344096 | tf_op jit(solution)/shard_map/ppermute | solution.py:14
  41.0 1.4 convolution_convert_fusion.1
  42.4 11.7 %all-to-all-done = bf16[16,16,1792]{2,1,0:T(8,128)(2,1)S(1)} async-done(((bf16[16,16,1792]{2,1,0:T(8,128)(2,1)}), bf16[16,16,1792]{2,1,0:T(8,128)(2,1)S(1)}, u32[]{:S(2)}, u32[]{:S(2)}) %all-to-all-start) | async-done | bytes 917536 | tf_op jit(solution)/shard_map/all_to_all | solution.py:31
  54.1 3.5 all-to-all-start.5
  59.9 22.9 %all-to-all-done.5 = bf16[16,16,1792]{2,1,0:T(8,128)(2,1)S(1)} async-done(((bf16[16,16,1792]{2,1,0:T(8,128)(2,1)}), bf16[16,16,1792]{2,1,0:T(8,128)(2,1)S(1)}, u32[]{:S(2)}, u32[]{:S(2)}) %all-to-all-start.5) | async-done | bytes 917536 | tf_op jit(solution)/shard_map/all_to_all | solution.py:31
  82.7 4.2 %all-to-all-start.4 = ((bf16[16,16,1792]{2,1,0:T(8,128)(2,1)}), bf16[16,16,1792]{2,1,0:T(8,128)(2,1)}, u32[]{:S(2)}, u32[]{:S(2)}) async-start(bf16[16,16,1792]{2,1,0:T(8,128)(2,1)} %bitcast.220), calls=%async_computation.4 | async-start | bytes 1835008 | tf_op jit(solution)/shard_map/all_to_all | solution.py:31
  87.0 4.3 %fusion.200 = (bf16[256,1024]{1,0:T(8,128)(2,1)S(1)}, f32[256,1024]{1,0:T(8,128)}) fusion(bf16[256,1792]{1,0:T(8,128)(2,1)S(1)} %bitcast.215, bf16[1,1,1792,1024]{3,2,1,0:T(8,128)(2,1)} %param.15), kind=kOutput, calls=%fused_computation.291 | convolution fusion | flops 939786240 | bytes 6160384 | tf_op jit(solution)/shard_map/dot_general | solution.py:40
  91.3 2.1 fusion.201
  94.7 2.1 fusion.205
  96.8 2.3 fusion.206
  99.2 12.3 %all-to-all-done.4 = bf16[16,16,1792]{2,1,0:T(8,128)(2,1)} async-done(((bf16[16,16,1792]{2,1,0:T(8,128)(2,1)}), bf16[16,16,1792]{2,1,0:T(8,128)(2,1)}, u32[]{:S(2)}, u32[]{:S(2)}) %all-to-all-start.4) | async-done | bytes 917536 | tf_op jit(solution)/shard_map/all_to_all | solution.py:31
  111.5 4.5 %fusion.204 = (bf16[256,1024]{1,0:T(8,128)(2,1)S(1)}, f32[256,1024]{1,0:T(8,128)}) fusion(bf16[256,1792]{1,0:T(8,128)(2,1)} %bitcast.45, bf16[1,1,1024,1792]{3,2,1,0:T(8,128)(2,1)} %param.16), kind=kOutput, calls=%fused_computation.295 | convolution fusion | flops 939786240 | bytes 6160384 | tf_op jit(solution)/shard_map/dot_general | solution.py:36
  116.4 5.1 %collective-permute-done.2 = bf16[256,2048]{1,0:T(8,128)(2,1)} collective-permute-done((bf16[256,2048]{1,0:T(8,128)(2,1)}, bf16[256,2048]{1,0:T(8,128)(2,1)}, u32[]{:S(2)}, u32[]{:S(2)}) %collective-permute-start.2) | collective-permute-done | bytes 1048608 | tf_op jit(solution)/shard_map/ppermute | solution.py:14
  121.5 1.4 convert_element_type.232
  123.0 2.3 fusion.44
  125.3 7.2 %all-to-all-start.1 = ((bf16[16,16,1792]{2,1,0:T(8,128)(2,1)}), bf16[16,16,1792]{2,1,0:T(8,128)(2,1)S(1)}, u32[]{:S(2)}, u32[]{:S(2)}) async-start(bf16[16,16,1792]{2,1,0:T(8,128)(2,1)} %bitcast.224), calls=%async_computation.1 | async-start | bytes 1835008 | tf_op jit(solution)/shard_map/all_to_all | solution.py:31
  132.5 22.3 %collective-permute-done.9 = bf16[256,3072]{1,0:T(8,128)(2,1)} collective-permute-done((bf16[256,3072]{1,0:T(8,128)(2,1)S(1)}, bf16[256,3072]{1,0:T(8,128)(2,1)}, u32[]{:S(2)}, u32[]{:S(2)}) %collective-permute-start.9) | collective-permute-done | bytes 1572896 | tf_op jit(solution)/shard_map/ppermute | solution.py:14
  154.9 1.8 convert_element_type.262
  156.7 2.8 fusion.12
  159.6 2.5 fusion.41
  162.1 6.8 %all-to-all-start.6 = ((bf16[16,16,1792]{2,1,0:T(8,128)(2,1)}), bf16[16,16,1792]{2,1,0:T(8,128)(2,1)S(1)}, u32[]{:S(2)}, u32[]{:S(2)}) async-start(bf16[16,16,1792]{2,1,0:T(8,128)(2,1)} %bitcast.221), calls=%async_computation.6 | async-start | bytes 1835008 | tf_op jit(solution)/shard_map/all_to_all | solution.py:31
  169.2 7.2 %collective-permute-done.13 = bf16[48,1792]{1,0:T(8,128)(2,1)S(1)} collective-permute-done((bf16[48,1792]{1,0:T(8,128)(2,1)S(1)}, bf16[48,1792]{1,0:T(8,128)(2,1)S(1)}, u32[]{:S(2)}, u32[]{:S(2)}) %collective-permute-start.13) | collective-permute-done | bytes 172064 | tf_op jit(solution)/shard_map/ppermute | solution.py:14
  177.4 1.4 convolution_convert_fusion
  178.9 15.3 %all-to-all-done.6 = bf16[16,16,1792]{2,1,0:T(8,128)(2,1)S(1)} async-done(((bf16[16,16,1792]{2,1,0:T(8,128)(2,1)}), bf16[16,16,1792]{2,1,0:T(8,128)(2,1)S(1)}, u32[]{:S(2)}, u32[]{:S(2)}) %all-to-all-start.6) | async-done | bytes 917536 | tf_op jit(solution)/shard_map/all_to_all | solution.py:31
  194.1 4.2 %all-to-all-start.8 = ((bf16[16,16,1792]{2,1,0:T(8,128)(2,1)}), bf16[16,16,1792]{2,1,0:T(8,128)(2,1)}, u32[]{:S(2)}, u32[]{:S(2)}) async-start(bf16[16,16,1792]{2,1,0:T(8,128)(2,1)} %bitcast.63), calls=%async_computation.8 | async-start | bytes 1835008 | tf_op jit(solution)/shard_map/all_to_all | solution.py:31
  199.2 2.3 collective-permute-start.4
  201.6 2.9 collective-permute-start.5
  204.5 3.1 collective-permute-start.3
  209.1 1.9 collective-permute-start.10
  211.1 6.1 %collective-permute-done.3 = bf16[96,1792]{1,0:T(8,128)(2,1)S(1)} collective-permute-done((bf16[96,1792]{1,0:T(8,128)(2,1)S(1)}, bf16[96,1792]{1,0:T(8,128)(2,1)S(1)}, u32[]{:S(2)}, u32[]{:S(2)}) %collective-permute-start.3) | collective-permute-done | bytes 344096 | tf_op jit(solution)/shard_map/ppermute | solution.py:26
  217.2 1.5 convolution_convert_fusion.2
  218.6 4.3 %all-to-all-done.8 = bf16[16,16,1792]{2,1,0:T(8,128)(2,1)} async-done(((bf16[16,16,1792]{2,1,0:T(8,128)(2,1)}), bf16[16,16,1792]{2,1,0:T(8,128)(2,1)}, u32[]{:S(2)}, u32[]{:S(2)}) %all-to-all-start.8) | async-done | bytes 917536 | tf_op jit(solution)/shard_map/all_to_all | solution.py:31
  222.9 4.2 %all-to-all-start.2 = ((bf16[16,16,1792]{2,1,0:T(8,128)(2,1)}), bf16[16,16,1792]{2,1,0:T(8,128)(2,1)}, u32[]{:S(2)}, u32[]{:S(2)}) async-start(bf16[16,16,1792]{2,1,0:T(8,128)(2,1)} %bitcast.29), calls=%async_computation.2 | async-start | bytes 1835008 | tf_op jit(solution)/shard_map/all_to_all | solution.py:31
  227.4 2.3 collective-permute-start.11
  229.7 9.5 %collective-permute-done.11 = bf16[96,1792]{1,0:T(8,128)(2,1)S(1)} collective-permute-done((bf16[96,1792]{1,0:T(8,128)(2,1)S(1)}, bf16[96,1792]{1,0:T(8,128)(2,1)S(1)}, u32[]{:S(2)}, u32[]{:S(2)}) %collective-permute-start.11) | collective-permute-done | bytes 344096 | tf_op jit(solution)/shard_map/ppermute | solution.py:26
  240.8 10.9 %all-to-all-done.2 = bf16[16,16,1792]{2,1,0:T(8,128)(2,1)} async-done(((bf16[16,16,1792]{2,1,0:T(8,128)(2,1)}), bf16[16,16,1792]{2,1,0:T(8,128)(2,1)}, u32[]{:S(2)}, u32[]{:S(2)}) %all-to-all-start.2) | async-done | bytes 917536 | tf_op jit(solution)/shard_map/all_to_all | solution.py:31
  251.7 3.5 all-to-all-start.7
  255.2 4.5 %fusion.202 = (bf16[256,1024]{1,0:T(8,128)(2,1)S(1)}, f32[256,1024]{1,0:T(8,128)}) fusion(bf16[256,1792]{1,0:T(8,128)(2,1)} %bitcast.30, bf16[1,1,1792,1024]{3,2,1,0:T(8,128)(2,1)} %param.15), kind=kOutput, calls=%fused_computation.293 | convolution fusion | flops 939786240 | bytes 6160384 | tf_op jit(solution)/shard_map/dot_general | solution.py:40
  259.8 3.5 fusion.203
  264.4 1.8 collective-permute-start.6
  266.1 3.3 fusion.208
  269.4 3.3 fusion.209
  275.1 5.2 %all-to-all-done.7 = bf16[16,16,1792]{2,1,0:T(8,128)(2,1)S(1)} async-done(((bf16[16,16,1792]{2,1,0:T(8,128)(2,1)}), bf16[16,16,1792]{2,1,0:T(8,128)(2,1)S(1)}, u32[]{:S(2)}, u32[]{:S(2)}) %all-to-all-start.7) | async-done | bytes 917536 | tf_op jit(solution)/shard_map/all_to_all | solution.py:31
  280.3 4.5 %fusion.207 = (bf16[256,1024]{1,0:T(8,128)(2,1)}, f32[256,1024]{1,0:T(8,128)}) fusion(bf16[256,1792]{1,0:T(8,128)(2,1)S(1)} %bitcast.219, bf16[1,1,1024,1792]{3,2,1,0:T(8,128)(2,1)} %param.16), kind=kOutput, calls=%fused_computation.298 | convolution fusion | flops 939786240 | bytes 6160384 | tf_op jit(solution)/shard_map/dot_general | solution.py:36
  284.8 1.8 collective-permute-start.12
  286.6 4.5 %collective-permute-done.6 = bf16[256,2048]{1,0:T(8,128)(2,1)} collective-permute-done((bf16[256,2048]{1,0:T(8,128)(2,1)}, bf16[256,2048]{1,0:T(8,128)(2,1)}, u32[]{:S(2)}, u32[]{:S(2)}) %collective-permute-start.6) | collective-permute-done | bytes 1048608 | tf_op jit(solution)/shard_map/ppermute | solution.py:14
  291.1 1.4 convert_element_type.244
  292.5 2.2 fusion.47
  294.8 8.1 %all-to-all-start.3 = ((bf16[16,16,1792]{2,1,0:T(8,128)(2,1)}), bf16[16,16,1792]{2,1,0:T(8,128)(2,1)S(1)}, u32[]{:S(2)}, u32[]{:S(2)}) async-start(bf16[16,16,1792]{2,1,0:T(8,128)(2,1)} %bitcast.223), calls=%async_computation.3 | async-start | bytes 1835008 | tf_op jit(solution)/shard_map/all_to_all | solution.py:31
  302.9 10.5 %collective-permute-done.14 = bf16[256,2048]{1,0:T(8,128)(2,1)S(1)} collective-permute-done((bf16[256,2048]{1,0:T(8,128)(2,1)}, bf16[256,2048]{1,0:T(8,128)(2,1)S(1)}, u32[]{:S(2)}, u32[]{:S(2)}) %collective-permute-start.14) | collective-permute-done | bytes 1048608 | tf_op jit(solution)/shard_map/ppermute | solution.py:14
  313.7 11.1 %collective-permute-done.12 = bf16[256,1024]{1,0:T(8,128)(2,1)} collective-permute-done((bf16[256,1024]{1,0:T(8,128)(2,1)}, bf16[256,1024]{1,0:T(8,128)(2,1)}, u32[]{:S(2)}, u32[]{:S(2)}) %collective-permute-start.12) | collective-permute-done | bytes 524320 | tf_op jit(solution)/shard_map/ppermute | solution.py:14
  324.8 3.7 fusion.8
  328.6 3.6 fusion.38
  332.2 7.4 %all-to-all-start.9 = ((bf16[16,16,1792]{2,1,0:T(8,128)(2,1)}), bf16[16,16,1792]{2,1,0:T(8,128)(2,1)S(1)}, u32[]{:S(2)}, u32[]{:S(2)}) async-start(bf16[16,16,1792]{2,1,0:T(8,128)(2,1)} %bitcast.222), calls=%async_computation.9 | async-start | bytes 1835008 | tf_op jit(solution)/shard_map/all_to_all | solution.py:31
  340.3 1.9 collective-permute-start.7
  342.2 22.7 %all-to-all-done.9 = bf16[16,16,1792]{2,1,0:T(8,128)(2,1)S(1)} async-done(((bf16[16,16,1792]{2,1,0:T(8,128)(2,1)}), bf16[16,16,1792]{2,1,0:T(8,128)(2,1)S(1)}, u32[]{:S(2)}, u32[]{:S(2)}) %all-to-all-start.9) | async-done | bytes 917536 | tf_op jit(solution)/shard_map/all_to_all | solution.py:31
  365.6 1.9 collective-permute-start.15
  367.5 2.1 collective-permute-done.15
  369.9 1.9 collective-permute-start.16
  372.5 5.3 %collective-permute-done.16 = bf16[48,1792]{1,0:T(8,128)(2,1)S(1)} collective-permute-done((bf16[48,1792]{1,0:T(8,128)(2,1)S(1)}, bf16[48,1792]{1,0:T(8,128)(2,1)S(1)}, u32[]{:S(2)}, u32[]{:S(2)}) %collective-permute-start.16) | collective-permute-done | bytes 172064 | tf_op jit(solution)/shard_map/ppermute | solution.py:14
  (144 shorter events, 26.3 us)
Async XLA Ops:
  0.6 9.1 %copy-start = (f32[1,3584]{1,0:T(1,128)S(1)}, f32[1,3584]{1,0:T(1,128)}, u32[]{:S(2)}) copy-start(f32[1,3584]{1,0:T(1,128)} %param.13) | copy-start | bytes 43012
  0.6 28.2 %copy-start.2 = (bf16[2,1,48,3584]{3,2,1,0:T(8,128)(2,1)S(1)}, bf16[2,1,48,3584]{3,2,1,0:T(8,128)(2,1)}, u32[]{:S(2)}) copy-start(bf16[2,1,48,3584]{3,2,1,0:T(8,128)(2,1)} %param.11) | copy-start | bytes 2064388
  2.0 27.5 %copy-start.3 = (bf16[1,48,3584]{2,1,0:T(8,128)(2,1)S(1)}, bf16[1,48,3584]{2,1,0:T(8,128)(2,1)}, u32[]{:S(2)}) copy-start(bf16[1,48,3584]{2,1,0:T(8,128)(2,1)} %param.12) | copy-start | bytes 1032196
  5.6 4.1 %collective-permute-start.1 = (f32[19,48]{1,0:T(8,128)S(1)}, f32[19,48]{1,0:T(8,128)S(1)}, u32[]{:S(2)}, u32[]{:S(2)}) collective-permute-start(f32[19,48]{1,0:T(8,128)S(1)} %concatenate.46), channel_id=1, source_target_pairs={{0,1},{1,0},{2,3},{3,2},{4,5},{5,4},{6,7},{7,6},{8,9},{9,8},{10,11... | collective-permute-start | bytes 10952 | tf_op jit(solution)/shard_map/ppermute | solution.py:14
  9.5 6.5 %collective-permute-start = (bf16[48,1792]{1,0:T(8,128)(2,1)S(1)}, bf16[48,1792]{1,0:T(8,128)(2,1)S(1)}, u32[]{:S(2)}, u32[]{:S(2)}) collective-permute-start(bf16[48,1792]{1,0:T(8,128)(2,1)S(1)} %dynamic-slice_bitcast_fusion.1), channel_id=1, source_target_pairs={{0,1},{1,0},{2,3},{3,2},{4,5},{5,4},{6,7},{7,6},{8,9},{9,8},{10,11... | collective-permute-start | bytes 516104 | tf_op jit(solution)/shard_map/ppermute | solution.py:14
  11.1 7.4 %copy-start.8 = (s32[96]{0:T(128)}, s32[96]{0:T(128)S(1)}, u32[]{:S(2)}) copy-start(s32[96]{0:T(128)S(1)} %get-tuple-element.38) | copy-start | bytes 1156
  11.1 7.4 %copy-start.12 = (s32[96]{0:T(128)}, s32[96]{0:T(128)S(1)}, u32[]{:S(2)}) copy-start(s32[96]{0:T(128)S(1)} %get-tuple-element.37) | copy-start | bytes 1156
  18.5 35.6 %all-to-all-start = ((bf16[16,16,1792]{2,1,0:T(8,128)(2,1)}), bf16[16,16,1792]{2,1,0:T(8,128)(2,1)S(1)}, u32[]{:S(2)}, u32[]{:S(2)}) async-start(bf16[16,16,1792]{2,1,0:T(8,128)(2,1)} %bitcast.16), calls=%async_computation | async-start | bytes 1835008 | tf_op jit(solution)/shard_map/all_to_all | solution.py:31
  29.6 11.2 %collective-permute-start.8 = (bf16[2,48,1792]{2,1,0:T(8,128)(2,1)S(1)}, bf16[2,48,1792]{2,1,0:T(8,128)(2,1)S(1)}, u32[]{:S(2)}, u32[]{:S(2)}) collective-permute-start(bf16[2,48,1792]{2,1,0:T(8,128)(2,1)S(1)} %fusion.118), channel_id=1, source_target_pairs={{0,1},{1,0},{2,3},{3,2},{4,5},{5,4},{6,7},{7,6},{8,9},{9,8},{10,11... | collective-permute-start | bytes 1032200 | tf_op jit(solution)/shard_map/ppermute | solution.py:14
  54.1 28.6 %all-to-all-start.5 = ((bf16[16,16,1792]{2,1,0:T(8,128)(2,1)}), bf16[16,16,1792]{2,1,0:T(8,128)(2,1)S(1)}, u32[]{:S(2)}, u32[]{:S(2)}) async-start(bf16[16,16,1792]{2,1,0:T(8,128)(2,1)} %bitcast.47), calls=%async_computation.5 | async-start | bytes 1835008 | tf_op jit(solution)/shard_map/all_to_all | solution.py:31
  82.7 28.8 %all-to-all-start.4 = ((bf16[16,16,1792]{2,1,0:T(8,128)(2,1)}), bf16[16,16,1792]{2,1,0:T(8,128)(2,1)}, u32[]{:S(2)}, u32[]{:S(2)}) async-start(bf16[16,16,1792]{2,1,0:T(8,128)(2,1)} %bitcast.220), calls=%async_computation.4 | async-start | bytes 1835008 | tf_op jit(solution)/shard_map/all_to_all | solution.py:31
  87.0 4.3 %copy-start.25 = (bf16[1,1,1792,1024]{3,2,1,0:T(8,128)(2,1)S(1)}, bf16[1,1,1792,1024]{3,2,1,0:T(8,128)(2,1)}, u32[]{:S(2)}) copy-start(bf16[1,1,1792,1024]{3,2,1,0:T(8,128)(2,1)} %param.14) | copy-start | bytes 11010052
  91.3 3.5 copy-start.22
  94.5 27.0 %collective-permute-start.2 = (bf16[256,2048]{1,0:T(8,128)(2,1)}, bf16[256,2048]{1,0:T(8,128)(2,1)}, u32[]{:S(2)}, u32[]{:S(2)}) collective-permute-start(bf16[256,2048]{1,0:T(8,128)(2,1)} %pad_maximum_fusion.1), channel_id=1, source_target_pairs={{0,1},{1,0},{2,3},{3,2},{4,5},{5,4},{6,7},{7,6},{8,9},{9,8},{10,11... | collective-permute-start | bytes 3145736 | tf_op jit(solution)/shard_map/ppermute | solution.py:14
  111.5 4.5 %copy-start.5 = (bf16[256,1024]{1,0:T(8,128)(2,1)S(1)}, bf16[256,1024]{1,0:T(8,128)(2,1)}, u32[]{:S(2)}) copy-start(bf16[256,1024]{1,0:T(8,128)(2,1)} %get-tuple-element.57) | copy-start | bytes 1572868
  116.0 7.0 %copy-start.20 = (bf16[1,1,1024,1792]{3,2,1,0:T(8,128)(2,1)S(1)}, bf16[1,1,1024,1792]{3,2,1,0:T(8,128)(2,1)}, u32[]{:S(2)}) copy-start(bf16[1,1,1024,1792]{3,2,1,0:T(8,128)(2,1)} %param.16) | copy-start | bytes 11010052
  116.0 7.0 %copy-start.35 = (f32[256,1024]{1,0:T(8,128)S(1)}, f32[256,1024]{1,0:T(8,128)}, u32[]{:S(2)}) copy-start(f32[256,1024]{1,0:T(8,128)} %get-tuple-element.44) | copy-start | bytes 3145732
  116.0 7.0 %copy-start.36 = (f32[256,1024]{1,0:T(8,128)S(1)}, f32[256,1024]{1,0:T(8,128)}, u32[]{:S(2)}) copy-start(f32[256,1024]{1,0:T(8,128)} %get-tuple-element.46) | copy-start | bytes 3145732
  116.1 38.8 %collective-permute-start.9 = (bf16[256,3072]{1,0:T(8,128)(2,1)S(1)}, bf16[256,3072]{1,0:T(8,128)(2,1)}, u32[]{:S(2)}, u32[]{:S(2)}) collective-permute-start(bf16[256,3072]{1,0:T(8,128)(2,1)S(1)} %pad_maximum_fusion), channel_id=1, source_target_pairs={{0,1},{1,0},{2,3},{3,2},{4,5},{5,4},{6,7},{7,6},{8,9},{9,8},{10,11... | collective-permute-start | bytes 4718600 | tf_op jit(solution)/shard_map/ppermute | solution.py:14
  125.3 36.8 %all-to-all-start.1 = ((bf16[16,16,1792]{2,1,0:T(8,128)(2,1)}), bf16[16,16,1792]{2,1,0:T(8,128)(2,1)S(1)}, u32[]{:S(2)}, u32[]{:S(2)}) async-start(bf16[16,16,1792]{2,1,0:T(8,128)(2,1)} %bitcast.224), calls=%async_computation.1 | async-start | bytes 1835008 | tf_op jit(solution)/shard_map/all_to_all | solution.py:31
  132.5 24.1 %copy-start.23 = (bf16[1,1,1792,1024]{3,2,1,0:T(8,128)(2,1)S(1)}, bf16[1,1,1792,1024]{3,2,1,0:T(8,128)(2,1)}, u32[]{:S(2)}) copy-start(bf16[1,1,1792,1024]{3,2,1,0:T(8,128)(2,1)} %param.15) | copy-start | bytes 11010052
  132.5 24.1 %copy-start.32 = (f32[256,1024]{1,0:T(8,128)S(1)}, f32[256,1024]{1,0:T(8,128)}, u32[]{:S(2)}) copy-start(f32[256,1024]{1,0:T(8,128)} %get-tuple-element.58) | copy-start | bytes 3145732
  156.7 2.9 copy-start.37
  159.6 9.3 %copy-start.4 = (bf16[1,1,48,3584]{3,2,1,0:T(8,128)(2,1)S(1)}, bf16[1,1,48,3584]{3,2,1,0:T(8,128)(2,1)}, u32[]{:S(2)}) copy-start(bf16[1,1,48,3584]{3,2,1,0:T(8,128)(2,1)} %get-tuple-element.6) | copy-start | bytes 1032196
  162.1 36.3 %copy-start.9 = (s32[96]{0:T(128)S(1)}, s32[96]{0:T(128)}, u32[]{:S(2)}) copy-start(s32[96]{0:T(128)} %copy-done.8) | copy-start | bytes 1156
  162.1 32.1 %all-to-all-start.6 = ((bf16[16,16,1792]{2,1,0:T(8,128)(2,1)}), bf16[16,16,1792]{2,1,0:T(8,128)(2,1)S(1)}, u32[]{:S(2)}, u32[]{:S(2)}) async-start(bf16[16,16,1792]{2,1,0:T(8,128)(2,1)} %bitcast.221), calls=%async_computation.6 | async-start | bytes 1835008 | tf_op jit(solution)/shard_map/all_to_all | solution.py:31
  168.8 29.9 %copy-start.13 = (s32[96]{0:T(128)S(1)}, s32[96]{0:T(128)}, u32[]{:S(2)}) copy-start(s32[96]{0:T(128)} %copy-done.12) | copy-start | bytes 1156
  168.9 29.9 %copy-start.18 = (f32[96]{0:T(128)S(1)}, f32[96]{0:T(128)}, u32[]{:S(2)}) copy-start(f32[96]{0:T(128)} %get-tuple-element.22) | copy-start | bytes 1156
  168.9 29.9 %copy-start.19 = (f32[96]{0:T(128)S(1)}, f32[96]{0:T(128)}, u32[]{:S(2)}) copy-start(f32[96]{0:T(128)} %get-tuple-element.26) | copy-start | bytes 1156
  168.9 7.5 %collective-permute-start.13 = (bf16[48,1792]{1,0:T(8,128)(2,1)S(1)}, bf16[48,1792]{1,0:T(8,128)(2,1)S(1)}, u32[]{:S(2)}, u32[]{:S(2)}) collective-permute-start(bf16[48,1792]{1,0:T(8,128)(2,1)S(1)} %dynamic-slice_bitcast_fusion), channel_id=1, source_target_pairs={{0,1},{1,0},{2,3},{3,2},{4,5},{5,4},{6,7},{7,6},{8,9},{9,8},{10,11... | collective-permute-start | bytes 516104 | tf_op jit(solution)/shard_map/ppermute | solution.py:14
  194.1 28.8 %all-to-all-start.8 = ((bf16[16,16,1792]{2,1,0:T(8,128)(2,1)}), bf16[16,16,1792]{2,1,0:T(8,128)(2,1)}, u32[]{:S(2)}, u32[]{:S(2)}) async-start(bf16[16,16,1792]{2,1,0:T(8,128)(2,1)} %bitcast.63), calls=%async_computation.8 | async-start | bytes 1835008 | tf_op jit(solution)/shard_map/all_to_all | solution.py:31
  198.7 18.4 %copy-start.6 = (s32[96]{0:T(128)S(1)}, s32[96]{0:T(128)}, u32[]{:S(2)}) copy-start(s32[96]{0:T(128)} %get-tuple-element.35) | copy-start | bytes 1156
  198.7 18.4 %copy-start.10 = (s32[96]{0:T(128)S(1)}, s32[96]{0:T(128)}, u32[]{:S(2)}) copy-start(s32[96]{0:T(128)} %get-tuple-element.36) | copy-start | bytes 1156
  199.2 8.3 %collective-permute-start.4 = (f32[1,96]{1,0:T(1,128)S(1)}, f32[1,96]{1,0:T(1,128)S(1)}, u32[]{:S(2)}, u32[]{:S(2)}) collective-permute-start(f32[1,96]{1,0:T(1,128)S(1)} %bitcast.231), channel_id=1, source_target_pairs={{0,32},{1,33},{32,64},{33,65},{64,96},{65,97},{96,128},{97,129},{1... | collective-permute-start | bytes 1160 | tf_op jit(solution)/shard_map/ppermute | solution.py:26
  201.6 6.8 %collective-permute-start.5 = (f32[1,96]{1,0:T(1,128)S(1)}, f32[1,96]{1,0:T(1,128)S(1)}, u32[]{:S(2)}, u32[]{:S(2)}) collective-permute-start(f32[1,96]{1,0:T(1,128)S(1)} %bitcast.232), channel_id=1, source_target_pairs={{0,33},{1,32},{32,65},{33,64},{64,97},{65,96},{96,129},{97,128},{1... | collective-permute-start | bytes 1160 | tf_op jit(solution)/shard_map/ppermute | solution.py:26
  204.5 12.7 %collective-permute-start.3 = (bf16[96,1792]{1,0:T(8,128)(2,1)S(1)}, bf16[96,1792]{1,0:T(8,128)(2,1)S(1)}, u32[]{:S(2)}, u32[]{:S(2)}) collective-permute-start(bf16[96,1792]{1,0:T(8,128)(2,1)S(1)} %get-tuple-element.48), channel_id=1, source_target_pairs={{0,32},{1,33},{32,64},{33,65},{64,96},{65,97},{96,128},{97,129},{1... | collective-permute-start | bytes 1032200 | tf_op jit(solution)/shard_map/ppermute | solution.py:26
  209.1 30.1 %copy-start.15 = (f32[96]{0:T(128)S(1)}, f32[96]{0:T(128)}, u32[]{:S(2)}) copy-start(f32[96]{0:T(128)} %get-tuple-element.39) | copy-start | bytes 1156
  209.1 30.1 %copy-start.16 = (f32[96]{0:T(128)S(1)}, f32[96]{0:T(128)}, u32[]{:S(2)}) copy-start(f32[96]{0:T(128)} %get-tuple-element.40) | copy-start | bytes 1156
  209.1 18.0 %collective-permute-start.10 = (f32[1,96]{1,0:T(1,128)S(1)}, f32[1,96]{1,0:T(1,128)S(1)}, u32[]{:S(2)}, u32[]{:S(2)}) collective-permute-start(f32[1,96]{1,0:T(1,128)S(1)} %bitcast.230), channel_id=1, source_target_pairs={{0,1},{1,0},{2,3},{3,2},{4,5},{5,4},{6,7},{7,6},{8,9},{9,8},{10,11... | collective-permute-start | bytes 1160 | tf_op jit(solution)/shard_map/ppermute | solution.py:14
  222.9 28.8 %all-to-all-start.2 = ((bf16[16,16,1792]{2,1,0:T(8,128)(2,1)}), bf16[16,16,1792]{2,1,0:T(8,128)(2,1)}, u32[]{:S(2)}, u32[]{:S(2)}) async-start(bf16[16,16,1792]{2,1,0:T(8,128)(2,1)} %bitcast.29), calls=%async_computation.2 | async-start | bytes 1835008 | tf_op jit(solution)/shard_map/all_to_all | solution.py:31
  227.4 11.8 %collective-permute-start.11 = (bf16[96,1792]{1,0:T(8,128)(2,1)S(1)}, bf16[96,1792]{1,0:T(8,128)(2,1)S(1)}, u32[]{:S(2)}, u32[]{:S(2)}) collective-permute-start(bf16[96,1792]{1,0:T(8,128)(2,1)S(1)} %fusion.95), channel_id=1, source_target_pairs={{32,0},{33,1},{64,32},{65,33},{96,64},{97,65},{128,96},{129,97},{1... | collective-permute-start | bytes 1032200 | tf_op jit(solution)/shard_map/ppermute | solution.py:26
  251.7 28.6 %all-to-all-start.7 = ((bf16[16,16,1792]{2,1,0:T(8,128)(2,1)}), bf16[16,16,1792]{2,1,0:T(8,128)(2,1)S(1)}, u32[]{:S(2)}, u32[]{:S(2)}) async-start(bf16[16,16,1792]{2,1,0:T(8,128)(2,1)} %bitcast.59), calls=%async_computation.7 | async-start | bytes 1835008 | tf_op jit(solution)/shard_map/all_to_all | solution.py:31
  255.2 4.6 %copy-start.27 = (bf16[1,1,1792,1024]{3,2,1,0:T(8,128)(2,1)S(1)}, bf16[1,1,1792,1024]{3,2,1,0:T(8,128)(2,1)}, u32[]{:S(2)}) copy-start(bf16[1,1,1792,1024]{3,2,1,0:T(8,128)(2,1)} %param.14) | copy-start | bytes 11010052
  259.8 6.4 %copy-start.24 = (bf16[1,1,1792,1024]{3,2,1,0:T(8,128)(2,1)S(1)}, bf16[1,1,1792,1024]{3,2,1,0:T(8,128)(2,1)}, u32[]{:S(2)}) copy-start(bf16[1,1,1792,1024]{3,2,1,0:T(8,128)(2,1)} %param.15) | copy-start | bytes 11010052
  264.4 26.7 %collective-permute-start.6 = (bf16[256,2048]{1,0:T(8,128)(2,1)}, bf16[256,2048]{1,0:T(8,128)(2,1)}, u32[]{:S(2)}, u32[]{:S(2)}) collective-permute-start(bf16[256,2048]{1,0:T(8,128)(2,1)} %pad_maximum_fusion.2), channel_id=1, source_target_pairs={{0,1},{1,0},{2,3},{3,2},{4,5},{5,4},{6,7},{7,6},{8,9},{9,8},{10,11... | collective-permute-start | bytes 3145736 | tf_op jit(solution)/shard_map/ppermute | solution.py:14
  273.9 39.5 %collective-permute-start.14 = (bf16[256,2048]{1,0:T(8,128)(2,1)}, bf16[256,2048]{1,0:T(8,128)(2,1)S(1)}, u32[]{:S(2)}, u32[]{:S(2)}) collective-permute-start(bf16[256,2048]{1,0:T(8,128)(2,1)} %pad_maximum_fusion.3), channel_id=1, source_target_pairs={{0,1},{1,0},{2,3},{3,2},{4,5},{5,4},{6,7},{7,6},{8,9},{9,8},{10,11... | collective-permute-start | bytes 3145736 | tf_op jit(solution)/shard_map/ppermute | solution.py:14
  280.3 12.2 %copy-start.21 = (bf16[1,1,1024,1792]{3,2,1,0:T(8,128)(2,1)S(1)}, bf16[1,1,1024,1792]{3,2,1,0:T(8,128)(2,1)}, u32[]{:S(2)}) copy-start(bf16[1,1,1024,1792]{3,2,1,0:T(8,128)(2,1)} %param.16) | copy-start | bytes 11010052
  284.8 7.7 %copy-start.33 = (f32[256,1024]{1,0:T(8,128)S(1)}, f32[256,1024]{1,0:T(8,128)}, u32[]{:S(2)}) copy-start(f32[256,1024]{1,0:T(8,128)} %get-tuple-element.50) | copy-start | bytes 3145732
  284.8 7.7 %copy-start.34 = (f32[256,1024]{1,0:T(8,128)S(1)}, f32[256,1024]{1,0:T(8,128)}, u32[]{:S(2)}) copy-start(f32[256,1024]{1,0:T(8,128)} %get-tuple-element.52) | copy-start | bytes 3145732
  284.8 39.9 %collective-permute-start.12 = (bf16[256,1024]{1,0:T(8,128)(2,1)}, bf16[256,1024]{1,0:T(8,128)(2,1)}, u32[]{:S(2)}, u32[]{:S(2)}) collective-permute-start(bf16[256,1024]{1,0:T(8,128)(2,1)} %get-tuple-element.61), channel_id=1, source_target_pairs={{0,1},{1,0},{2,3},{3,2},{4,5},{5,4},{6,7},{7,6},{8,9},{9,8},{10,11... | collective-permute-start | bytes 1572872 | tf_op jit(solution)/shard_map/ppermute | solution.py:14
  294.8 37.4 %all-to-all-start.3 = ((bf16[16,16,1792]{2,1,0:T(8,128)(2,1)}), bf16[16,16,1792]{2,1,0:T(8,128)(2,1)S(1)}, u32[]{:S(2)}, u32[]{:S(2)}) async-start(bf16[16,16,1792]{2,1,0:T(8,128)(2,1)} %bitcast.223), calls=%async_computation.3 | async-start | bytes 1835008 | tf_op jit(solution)/shard_map/all_to_all | solution.py:31
  302.9 21.8 %copy-start.30 = (f32[256,1024]{1,0:T(8,128)S(1)}, f32[256,1024]{1,0:T(8,128)}, u32[]{:S(2)}) copy-start(f32[256,1024]{1,0:T(8,128)} %get-tuple-element.66) | copy-start | bytes 3145732
  302.9 21.8 %copy-start.38 = (f32[256,1024]{1,0:T(8,128)S(1)}, f32[256,1024]{1,0:T(8,128)}, u32[]{:S(2)}) copy-start(f32[256,1024]{1,0:T(8,128)} %get-tuple-element.62) | copy-start | bytes 3145732
  324.8 3.7 copy-start.28
  324.8 3.7 copy-start.29
  328.5 11.0 %copy-start.7 = (s32[96]{0:T(128)S(1)}, s32[96]{0:T(128)}, u32[]{:S(2)}) copy-start(s32[96]{0:T(128)} %get-tuple-element.35) | copy-start | bytes 1156
  328.5 11.0 %copy-start.14 = (f32[96]{0:T(128)S(1)}, f32[96]{0:T(128)}, u32[]{:S(2)}) copy-start(f32[96]{0:T(128)} %get-tuple-element.24) | copy-start | bytes 1156
  332.2 7.7 %copy-start.11 = (s32[96]{0:T(128)S(1)}, s32[96]{0:T(128)}, u32[]{:S(2)}) copy-start(s32[96]{0:T(128)} %get-tuple-element.36) | copy-start | bytes 1156
  332.2 7.7 %copy-start.17 = (f32[96]{0:T(128)S(1)}, f32[96]{0:T(128)}, u32[]{:S(2)}) copy-start(f32[96]{0:T(128)} %get-tuple-element.23) | copy-start | bytes 1156
  332.2 32.7 %all-to-all-start.9 = ((bf16[16,16,1792]{2,1,0:T(8,128)(2,1)}), bf16[16,16,1792]{2,1,0:T(8,128)(2,1)S(1)}, u32[]{:S(2)}, u32[]{:S(2)}) async-start(bf16[16,16,1792]{2,1,0:T(8,128)(2,1)} %bitcast.222), calls=%async_computation.9 | async-start | bytes 1835008 | tf_op jit(solution)/shard_map/all_to_all | solution.py:31
  340.3 27.2 %collective-permute-start.7 = (bf16[48,1792]{1,0:T(8,128)(2,1)S(1)}, bf16[48,1792]{1,0:T(8,128)(2,1)S(1)}, u32[]{:S(2)}, u32[]{:S(2)}) collective-permute-start(bf16[48,1792]{1,0:T(8,128)(2,1)S(1)} %broadcast_select_fusion.8), channel_id=1, source_target_pairs={{0,1},{1,0},{2,3},{3,2},{4,5},{5,4},{6,7},{7,6},{8,9},{9,8},{10,11... | collective-permute-start | bytes 516104 | tf_op jit(solution)/shard_map/ppermute | solution.py:14
  365.2 13.5 %copy-start.1 = (f32[1,3584]{1,0:T(1,128)S(1)}, f32[1,3584]{1,0:T(1,128)}, u32[]{:S(2)}) copy-start(f32[1,3584]{1,0:T(1,128)} %param.13) | copy-start | bytes 43012
  365.6 4.0 %collective-permute-start.15 = (f32[1,96]{1,0:T(1,128)S(1)}, f32[1,96]{1,0:T(1,128)S(1)}, u32[]{:S(2)}, u32[]{:S(2)}) collective-permute-start(f32[1,96]{1,0:T(1,128)S(1)} %bitcast.229), channel_id=1, source_target_pairs={{0,1},{1,0},{2,3},{3,2},{4,5},{5,4},{6,7},{7,6},{8,9},{9,8},{10,11... | collective-permute-start | bytes 1160 | tf_op jit(solution)/shard_map/ppermute | solution.py:14
  369.9 7.9 %collective-permute-start.16 = (bf16[48,1792]{1,0:T(8,128)(2,1)S(1)}, bf16[48,1792]{1,0:T(8,128)(2,1)S(1)}, u32[]{:S(2)}, u32[]{:S(2)}) collective-permute-start(bf16[48,1792]{1,0:T(8,128)(2,1)S(1)} %broadcast_select_fusion.4), channel_id=1, source_target_pairs={{0,1},{1,0},{2,3},{3,2},{4,5},{5,4},{6,7},{7,6},{8,9},{9,8},{10,11... | collective-permute-start | bytes 516104 | tf_op jit(solution)/shard_map/ppermute | solution.py:14
  (2 other events, 5.6 us)

commit v2 on v1

v2 whole, which is shorter than its diff:
```python
import jax
import jax.numpy as jnp
from jax import lax
from jax.sharding import PartitionSpec as P

ROUTE_SCALE = 2.5
EPSILON = 1e-06
BLOCK = 8
GROUP = 2 * BLOCK
BF16 = jnp.bfloat16
F32 = jnp.float32


def swap_dp(value):
    return lax.ppermute(value, "dp", [(0, 1), (1, 0)])


def move_section(value, step, flip_dp=False):
    sections = lax.axis_size("section")
    halves = lax.axis_size("dp")
    route = []
    for s in range(sections):
        if 0 <= s + step < sections:
            for d in range(halves):
                to = 1 - d if flip_dp else d
                route.append((s * halves + d, (s + step) * halves + to))
    return lax.ppermute(value, ("section", "dp"), route)


def route_rows(rows, axes="expert"):
    devices = lax.axis_size(axes)
    groups = rows.reshape(devices, -1, rows.shape[-1])
    moved = lax.all_to_all(groups, axes, split_axis=0, concat_axis=0, tiled=True)
    return moved.reshape(rows.shape)


def after(value, *earlier):
    return lax.optimization_barrier((value, *earlier))[0]


def contract_last(left, right):
    return lax.dot_general(left, right, (((1,), (1,)), ((), ())), preferred_element_type=F32)


def matmul(left, right):
    return jnp.dot(left, right, preferred_element_type=F32)


def pick(selector, rows):
    return lax.dot_general(selector, rows, (((0,), (0,)), ((), ())), preferred_element_type=F32)


def body(
    fwd_input,
    back_saved,
    back_grad,
    norm_gain,
    gate_weight,
    up_weight,
    down_weight,
    routes,
    slots,
    affinity,
):
    experts = lax.axis_size("expert")
    tokens = fwd_input.shape[1]
    width = fwd_input.shape[2]
    half = width // 2
    row_count = experts * GROUP
    side = lax.axis_index("dp")
    gate_w, up_w, down_w = gate_weight[0, 0], up_weight[0, 0], down_weight[0, 0]
    gain = norm_gain[0]
    gain_half = lax.dynamic_slice(gain, (side * half,), (half,))

    x0, s0, s1, g0 = fwd_input[0], back_saved[0, 0], back_saved[1, 0], back_grad[0]

    def inverse_of(value):
        wide = value.astype(F32)
        return lax.rsqrt(jnp.mean(wide * wide, axis=-1) + EPSILON)

    def in_order(own, other):
        return jnp.where(side == 0, own, other), jnp.where(side == 0, other, own)

    def split_halves(value):
        own = lax.dynamic_slice_in_dim(value, side * half, half, axis=-1)
        other = lax.dynamic_slice_in_dim(value, (1 - side) * half, half, axis=-1)
        return own, other

    def selector(marks):
        rows = lax.broadcasted_iota(jnp.int32, (row_count, marks.shape[-1]), 0)
        return (rows == marks[None, :]).astype(BF16)

    local = jnp.transpose(routes[:, 0] * GROUP + slots[:, 0], (0, 2, 1))
    local_mix = jnp.transpose(
        affinity[:, 0] / jnp.sum(affinity[:, 0], axis=-1, keepdims=True), (0, 2, 1)
    )

    def normed_of(value, inverse, scale):
        return (value.astype(F32) * inverse[:, None] * scale).astype(BF16)

    def spread(index, value):
        sides = [
            sum(selector(local[index, k] + h * BLOCK) for k in range(2)) for h in range(2)
        ]
        return matmul(
            jnp.concatenate(sides, axis=1),
            jnp.concatenate([value[:, :half], value[:, half:]], axis=0),
        ).astype(BF16)

    def gather_home(index, rows):
        return [
            jnp.concatenate(
                [pick(selector(local[index, k] + h * BLOCK), rows) for h in range(2)], axis=1
            )
            for k in range(2)
        ]

    scalars = jnp.concatenate(
        [
            jnp.stack([inverse_of(s0), inverse_of(s1)]),
            (local + side * BLOCK).astype(F32).reshape(8, tokens),
            local_mix.reshape(8, tokens),
        ]
    )
    table = jnp.concatenate(in_order(scalars, swap_dp(scalars)), axis=1)
    inverses = table[:2]
    marks = table[2:10].astype(jnp.int32).reshape(4, 2, -1)
    mixes = table[10:].reshape(4, 2, -1)

    def place_same(index, value):
        return matmul(selector(marks[index, 0]) + selector(marks[index, 1]), value).astype(BF16)

    def place_pair(index, pair):
        both = jnp.concatenate([selector(marks[index, k]) for k in range(2)], axis=1)
        return matmul(both, jnp.concatenate(pair, axis=0)).astype(BF16)

    def dp_sum(parts):
        sent = jnp.concatenate([part.astype(BF16) for part in parts], axis=1)
        got = swap_dp(sent).astype(F32)
        hidden = parts[0].shape[1]
        return [p + got[:, i * hidden : (i + 1) * hidden] for i, p in enumerate(parts)]

    def gate_up_parts(rows):
        return [matmul(rows, gate_w), matmul(rows, up_w)]

    def forward_rest(gate, upper):
        active = (gate * jax.nn.sigmoid(gate) * upper).astype(BF16)
        return matmul(active, down_w).astype(BF16)

    def backward_rest(gate, upper, dactive):
        sigma = jax.nn.sigmoid(gate)
        dgate = (dactive * upper * sigma * (1.0 + gate * (1.0 - sigma))).astype(BF16)
        dupper = (dactive * gate * sigma).astype(BF16)
        return (contract_last(dgate, gate_w) + contract_last(dupper, up_w)).astype(BF16)

    def forward_result(value, mix, picked):
        total = mix[0][:, None] * picked[0] + mix[1][:, None] * picked[1]
        return (value.astype(F32) + ROUTE_SCALE * total).astype(BF16)

    def sent_pair(index, grads):
        wide = grads.astype(F32)
        return [
            (ROUTE_SCALE * mixes[index, k][:, None] * wide).astype(BF16) for k in range(2)
        ]

    def backward_result(saved, inverse, grads, weighted, project):
        inv = inverse[:, None]
        return (
            grads.astype(F32)
            + inv * (weighted - saved.astype(F32) * inv * inv * project)
        ).astype(BF16)

    def pick_both(index, rows):
        return [pick(selector(marks[index, k]), rows) for k in range(2)]

    def side_by_side(first, second):
        shape = (experts, GROUP, half)
        joined = jnp.concatenate([first.reshape(shape), second.reshape(shape)], axis=1)
        moved = route_rows(joined.reshape(-1, half)).reshape(experts, 2 * GROUP, half)
        return moved[:, :GROUP].reshape(-1, half), moved[:, GROUP:].reshape(-1, half)

    def swap_halves(values):
        own, other = split_halves(jnp.stack(values))
        a, b = in_order(own, swap_dp(other))
        joined = jnp.concatenate([a, b], axis=1)
        return [joined[i] for i in range(len(values))]

    both_sides = ("expert", "dp")
    x0_sent = spread(0, normed_of(x0, inverse_of(x0), gain))
    x0_rows = route_rows(x0_sent, both_sides)
    s0h, g0h = swap_halves([s0, g0])
    x0h, s1h = swap_halves([x0, s1])
    s0_sent = place_same(1, normed_of(s0h, inverses[0], gain_half))
    g0_sent = place_pair(1, sent_pair(1, g0h))
    s0_sent = after(s0_sent, x0_rows)
    s0_rows, g0_rows = side_by_side(s0_sent, g0_sent)
    out0 = forward_rest(*dp_sum(gate_up_parts(x0_rows)))
    s1_sent = place_same(3, normed_of(s1h, inverses[1], gain_half))
    s1_sent = after(s1_sent, s0_rows)
    out0_back, s1_rows = side_by_side(out0, s1_sent)
    dexp0 = backward_rest(
        *dp_sum(gate_up_parts(s0_rows) + [contract_last(g0_rows, down_w)])
    )
    dexp0 = after(dexp0, out0_back)
    dexp0_back = route_rows(dexp0)

    first_out = forward_result(x0h, mixes[0], pick_both(0, out0_back))
    wide_out = first_out.astype(F32)
    square = jnp.sum(wide_out * wide_out, axis=-1)[None]
    x2h = move_section(first_out, 1)
    square_own = move_section(square, 1)
    square_other = move_section(square, 1, flip_dp=True)
    inverse2 = lax.rsqrt((square_own + square_other)[0] / width + EPSILON)
    x2_sent = place_same(2, normed_of(x2h, inverse2, gain_half))
    x2_sent = after(x2_sent, dexp0_back)
    x2_rows = route_rows(x2_sent)
    gate1, upper1 = dp_sum(gate_up_parts(s1_rows))

    back_picked = pick_both(1, dexp0_back)
    weighted = (back_picked[0] + back_picked[1]) * gain_half
    part = jnp.sum(weighted * s0h.astype(F32), axis=-1)[None]
    project = ((part + swap_dp(part)) / width)[0][:, None]
    first_back = backward_result(s0h, inverses[0], g0h, weighted, project)
    g3h = move_section(first_back, -1)
    g3_sent = place_pair(3, sent_pair(3, g3h))
    g3_sent = after(g3_sent, x2_rows)
    g3_rows = route_rows(g3_sent)

    def full_features(value):
        mine, theirs = in_order(value[:tokens], value[tokens:])
        return jnp.concatenate(in_order(mine, swap_dp(theirs)), axis=1)

    x2 = full_features(x2h)
    g3 = full_features(g3h)
    out2 = forward_rest(*dp_sum(gate_up_parts(x2_rows)))
    out2 = after(out2, g3_rows)
    out2_back = route_rows(out2, both_sides)
    (dactive1,) = dp_sum([contract_last(g3_rows, down_w)])
    dexp1 = backward_rest(gate1, upper1, dactive1)
    dexp1 = after(dexp1, out2_back)
    dexp1_back = route_rows(dexp1, both_sides)

    final_out = forward_result(x2, local_mix[2], gather_home(2, out2_back))
    back_picked = gather_home(3, dexp1_back)
    weighted = (back_picked[0] + back_picked[1]) * gain
    project = jnp.mean(weighted * s1.astype(F32), axis=-1, keepdims=True)
    final_back = backward_result(s1, inverse_of(s1), g3, weighted, project)
    return (final_out[None], final_back[None])


def solution(mesh):
    placed = (
        P("section", ("expert", "dp"), None),
        P(None, "section", ("expert", "dp"), None),
        P("section", ("expert", "dp"), None),
        P("section", None),
        P("section", "expert", "dp", None),
        P("section", "expert", "dp", None),
        P("section", "expert", None, "dp"),
        P(None, "section", ("expert", "dp"), None),
        P(None, "section", ("expert", "dp"), None),
        P(None, "section", ("expert", "dp"), None),
    )
    return jax.shard_map(
        body,
        mesh=mesh,
        in_specs=placed,
        out_specs=(P("section", ("expert", "dp"), None), P("section", ("expert", "dp"), None)),
        check_vma=False,
    )
```

time: 381 us -> 355 us (0.932)
  waiting for transfers between devices: 206 us -> 186 us
  matrix products: 63.2 us -> 55.8 us
    all_to_all x10 -> x8, waiting for transfers between devices: 105 us -> 65.8 us  [route_rows(): lax.all_to_all(groups, axes, split_axis=0, concat_axis=0, tiled=True)]
    ppermute x13 -> x11, waiting for transfers between devices: 84.1 us -> 105 us  [swap_dp(): return lax.ppermute(value, 'dp', [(0, 1), (1, 0)])]
    dot_general x16, matrix products: 38.6 us -> 33.6 us  [matmul(): return jnp.dot(left, right, preferred_element_type=F32)]
    all_to_all x10 -> x8, starting transfers between devices: 59.5 us -> 54.8 us  [route_rows(): lax.all_to_all(groups, axes, split_axis=0, concat_axis=0, tiled=True)]
    dot_general x6, matrix products: 21.6 us -> 17 us  [contract_last(): lax.dot_general(left, right, (((1,), (1,)), ((), ())), preferred_element_...]
    ppermute x13 -> x11, starting transfers between devices: 16.5 us -> 19.4 us  [swap_dp(): return lax.ppermute(value, 'dp', [(0, 1), (1, 0)])]
  transfers between devices with their start and end apart: 27 -> 23, of which waited for: 21 -> 13; matrix products, arithmetic and copies ran while one was open for 20% -> 16% of each run, Pallas kernels for 0% -> 0%
where the time goes in v2:
time: 355 us; the launch traced here: 354 us
  waiting for transfers between devices  186 us (52%)
  starting transfers between devices  86.2 us (24%)
  matrix products  55.8 us (16%)
  other arithmetic  18.4 us (5%)
  local copies, waits for them, and re-layouts  6.23 us (2%)
    ppermute x11, waiting for transfers between devices, swap_dp(): return lax.ppermute(value, 'dp', [(0, 1), (1, 0)])  105 us
    all_to_all x8, waiting for transfers between devices, route_rows(): lax.all_to_all(groups, axes, split_axis=0, concat_axis=0, tiled=True)  65.8 us
    all_to_all x8, starting transfers between devices, route_rows(): lax.all_to_all(groups, axes, split_axis=0, concat_axis=0, tiled=True)  54.8 us
    dot_general x16, matrix products, matmul(): return jnp.dot(left, right, preferred_element_type=F32)  33.6 us
    ppermute x11, starting transfers between devices, swap_dp(): return lax.ppermute(value, 'dp', [(0, 1), (1, 0)])  19.4 us
    dot_general x6, matrix products, contract_last(): lax.dot_general(left, right, (((1,), (1,)), ((), ())), preferred_element_...  17 us
    ppermute x4, waiting for transfers between devices, move_section(): return lax.ppermute(value, ('section', 'dp'), route)  14.8 us
    ppermute x4, starting transfers between devices, move_section(): return lax.ppermute(value, ('section', 'dp'), route)  12.1 us
  transfers between devices with their start and end apart: 23, of which 13 were waited for; matrix products, arithmetic and copies ran while one was open for 16% of the time, Pallas kernels for 0%

profile of v2, /device:TPU:3, one launch (start us, length us, event | category | flops | bytes accessed | tf_op | source)
XLA Modules:
  0.0 353.8 jit_solution(1919687506980645483)
XLA Ops:
  0.7 1.2 slice_bitcast_fusion
  1.9 1.7 fusion.124
  3.6 2.9 collective-permute-start.3
  6.5 1.7 fusion.126
  9.2 3.0 collective-permute-start.1
  12.7 1.4 fusion.50
  14.1 10.1 %all-to-all-start = ((bf16[32,8,1792]{2,1,0:T(8,128)(2,1)}), bf16[32,8,1792]{2,1,0:T(8,128)(2,1)S(1)}, u32[]{:S(2)}, u32[]{:S(2)}) async-start(bf16[32,8,1792]{2,1,0:T(8,128)(2,1)} %fusion.50), calls=%async_computation | async-start | bytes 1835008 | tf_op jit(solution)/shard_map/all_to_all | solution.py:33
  25.2 2.1 broadcast_select_fusion.1
  28.3 1.5 pad_maximum_fusion
  29.8 20.2 %all-to-all-done = bf16[32,8,1792]{2,1,0:T(8,128)(2,1)S(1)} async-done(((bf16[32,8,1792]{2,1,0:T(8,128)(2,1)}), bf16[32,8,1792]{2,1,0:T(8,128)(2,1)S(1)}, u32[]{:S(2)}, u32[]{:S(2)}) %all-to-all-start) | async-done | bytes 917536 | tf_op jit(solution)/shard_map/all_to_all | solution.py:33
  50.0 5.3 %all-to-all-start.1 = ((bf16[16,32,1792]{2,1,0:T(8,128)(2,1)}), bf16[16,32,1792]{2,1,0:T(8,128)(2,1)S(1)}, u32[]{:S(2)}, u32[]{:S(2)}) async-start(bf16[16,32,1792]{2,1,0:T(8,128)(2,1)} %pad_maximum_fusion), calls=%async_computation.1 | async-start | bytes 3670016 | tf_op jit(solution)/shard_map/all_to_all | solution.py:33
  55.2 3.3 fusion.221
  58.6 1.1 fusion.222
  59.8 2.0 collective-permute-start.2
  62.3 23.8 %collective-permute-done.2 = bf16[256,2048]{1,0:T(8,128)(2,1)S(1)} collective-permute-done((bf16[256,2048]{1,0:T(8,128)(2,1)S(1)}, bf16[256,2048]{1,0:T(8,128)(2,1)S(1)}, u32[]{:S(2)}, u32[]{:S(2)}) %collective-permute-start.2) | collective-permute-done | bytes 1048608 | tf_op jit(solution)/shard_map/ppermute | solution.py:15
  86.4 2.3 fusion.44
  88.7 10.2 %all-to-all-done.1 = bf16[16,32,1792]{2,1,0:T(8,128)(2,1)S(1)} async-done(((bf16[16,32,1792]{2,1,0:T(8,128)(2,1)}), bf16[16,32,1792]{2,1,0:T(8,128)(2,1)S(1)}, u32[]{:S(2)}, u32[]{:S(2)}) %all-to-all-start.1) | async-done | bytes 1835040 | tf_op jit(solution)/shard_map/all_to_all | solution.py:33
  99.9 1.3 copy-done.20
  101.2 2.3 fusion.224
  103.5 2.3 fusion.225
  105.8 1.5 pad_maximum_fusion.1
  107.3 4.8 %all-to-all-start.2 = ((bf16[16,32,1792]{2,1,0:T(8,128)(2,1)}), bf16[16,32,1792]{2,1,0:T(8,128)(2,1)S(1)}, u32[]{:S(2)}, u32[]{:S(2)}) async-start(bf16[16,32,1792]{2,1,0:T(8,128)(2,1)} %pad_maximum_fusion.1), calls=%async_computation.2 | async-start | bytes 3670016 | tf_op jit(solution)/shard_map/all_to_all | solution.py:33
  112.1 3.3 fusion.223
  115.5 2.1 collective-permute-start.8
  117.6 35.4 %collective-permute-done.8 = bf16[256,3072]{1,0:T(8,128)(2,1)S(1)} collective-permute-done((bf16[256,3072]{1,0:T(8,128)(2,1)S(1)}, bf16[256,3072]{1,0:T(8,128)(2,1)S(1)}, u32[]{:S(2)}, u32[]{:S(2)}) %collective-permute-start.8) | collective-permute-done | bytes 1572896 | tf_op jit(solution)/shard_map/ppermute | solution.py:15
  153.4 1.4 fusion.14
  155.7 2.4 fusion.41
  158.1 1.1 fusion.218
  159.2 7.8 %all-to-all-start.3 = ((bf16[16,16,1792]{2,1,0:T(8,128)(2,1)}), bf16[16,16,1792]{2,1,0:T(8,128)(2,1)S(1)}, u32[]{:S(2)}, u32[]{:S(2)}) async-start(bf16[16,16,1792]{2,1,0:T(8,128)(2,1)} %bitcast.292), calls=%async_computation.3 | async-start | bytes 1835008 | tf_op jit(solution)/shard_map/all_to_all | solution.py:33
  167.4 1.5 multiply_reduce_fusion
  168.9 3.0 collective-permute-start.6
  171.9 4.0 %collective-permute-start.7 = (f32[1,96]{1,0:T(1,128)S(1)}, f32[1,96]{1,0:T(1,128)S(1)}, u32[]{:S(2)}, u32[]{:S(2)}) collective-permute-start(f32[1,96]{1,0:T(1,128)S(1)} %bitcast.301), channel_id=1, source_target_pairs={{0,33},{1,32},{32,65},{33,64},{64,97},{65,96},{96,129},{97,128},{1... | collective-permute-start | bytes 1160 | tf_op jit(solution)/shard_map/ppermute | solution.py:27
  175.9 3.0 collective-permute-start.4
  179.0 8.7 %collective-permute-done.4 = bf16[96,1792]{1,0:T(8,128)(2,1)S(1)} collective-permute-done((bf16[96,1792]{1,0:T(8,128)(2,1)S(1)}, bf16[96,1792]{1,0:T(8,128)(2,1)S(1)}, u32[]{:S(2)}, u32[]{:S(2)}) %collective-permute-start.4) | collective-permute-done | bytes 344096 | tf_op jit(solution)/shard_map/ppermute | solution.py:27
  187.7 1.4 convolution_convert_fusion
  189.1 3.2 all-to-all-done.3
  192.7 5.1 %all-to-all-start.4 = ((bf16[16,16,1792]{2,1,0:T(8,128)(2,1)}), bf16[16,16,1792]{2,1,0:T(8,128)(2,1)}, u32[]{:S(2)}, u32[]{:S(2)}) async-start(bf16[16,16,1792]{2,1,0:T(8,128)(2,1)} %bitcast.57), calls=%async_computation.4 | async-start | bytes 1835008 | tf_op jit(solution)/shard_map/all_to_all | solution.py:33
  198.3 1.2 collective-permute-start.10
  199.5 2.8 collective-permute-done.10
  202.5 2.0 collective-permute-start.11
  204.6 2.1 fusion.230
  206.7 6.0 %collective-permute-done.11 = bf16[96,1792]{1,0:T(8,128)(2,1)S(1)} collective-permute-done((bf16[96,1792]{1,0:T(8,128)(2,1)S(1)}, bf16[96,1792]{1,0:T(8,128)(2,1)S(1)}, u32[]{:S(2)}, u32[]{:S(2)}) %collective-permute-start.11) | collective-permute-done | bytes 344096 | tf_op jit(solution)/shard_map/ppermute | solution.py:27
  212.9 1.4 convolution_convert_fusion.4
  214.3 8.9 %all-to-all-done.4 = bf16[16,16,1792]{2,1,0:T(8,128)(2,1)} async-done(((bf16[16,16,1792]{2,1,0:T(8,128)(2,1)}), bf16[16,16,1792]{2,1,0:T(8,128)(2,1)}, u32[]{:S(2)}, u32[]{:S(2)}) %all-to-all-start.4) | async-done | bytes 917536 | tf_op jit(solution)/shard_map/all_to_all | solution.py:33
  223.2 4.7 %fusion.226 = (bf16[256,1024]{1,0:T(8,128)(2,1)}, f32[256,1024]{1,0:T(8,128)}) fusion(bf16[256,1792]{1,0:T(8,128)(2,1)} %bitcast.58, bf16[1,1,1792,1024]{3,2,1,0:T(8,128)(2,1)} %param.15), kind=kOutput, calls=%fused_computation.348 | convolution fusion | flops 939786240 | bytes 6160384 | tf_op jit(solution)/shard_map/dot_general | solution.py:46
  227.9 3.5 fusion.227
  231.4 3.7 %all-to-all-start.5 = ((bf16[16,16,1792]{2,1,0:T(8,128)(2,1)}), bf16[16,16,1792]{2,1,0:T(8,128)(2,1)S(1)}, u32[]{:S(2)}, u32[]{:S(2)}) async-start(bf16[16,16,1792]{2,1,0:T(8,128)(2,1)} %bitcast.64), calls=%async_computation.5 | async-start | bytes 1835008 | tf_op jit(solution)/shard_map/all_to_all | solution.py:33
  235.1 1.3 pad_maximum_fusion.4
  236.4 1.3 collective-permute-start.9
  237.7 4.1 %fusion.229 = (bf16[256,1024]{1,0:T(8,128)(2,1)S(1)}, f32[256,1024]{1,0:T(8,128)}) fusion(bf16[256,1792]{1,0:T(8,128)(2,1)S(1)} %bitcast.286, bf16[1,1,1792,1024]{3,2,1,0:T(8,128)(2,1)} %param.15), kind=kOutput, calls=%fused_computation.351 | convolution fusion | flops 939786240 | bytes 6160384 | tf_op jit(solution)/shard_map/dot_general | solution.py:46
  241.8 1.1 pad_maximum_fusion.5
  242.9 2.0 collective-permute-start.14
  246.0 17.1 %collective-permute-done.9 = bf16[256,2048]{1,0:T(8,128)(2,1)S(1)} collective-permute-done((bf16[256,2048]{1,0:T(8,128)(2,1)S(1)}, bf16[256,2048]{1,0:T(8,128)(2,1)S(1)}, u32[]{:S(2)}, u32[]{:S(2)}) %collective-permute-start.9) | collective-permute-done | bytes 1048608 | tf_op jit(solution)/shard_map/ppermute | solution.py:15
  263.4 2.3 fusion.47
  265.6 4.3 %fusion.228 = (bf16[256,1024]{1,0:T(8,128)(2,1)}, f32[256,1024]{1,0:T(8,128)}) fusion(bf16[256,1792]{1,0:T(8,128)(2,1)S(1)} %bitcast.293, bf16[1,1,1024,1792]{3,2,1,0:T(8,128)(2,1)} %param.16), kind=kOutput, calls=%fused_computation.350 | convolution fusion | flops 939786240 | bytes 6160384 | tf_op jit(solution)/shard_map/dot_general | solution.py:42
  269.9 9.0 %all-to-all-start.6 = ((bf16[32,8,1792]{2,1,0:T(8,128)(2,1)}), bf16[32,8,1792]{2,1,0:T(8,128)(2,1)S(1)}, u32[]{:S(2)}, u32[]{:S(2)}) async-start(bf16[32,8,1792]{2,1,0:T(8,128)(2,1)} %bitcast.66), calls=%async_computation.6 | async-start | bytes 1835008 | tf_op jit(solution)/shard_map/all_to_all | solution.py:33
  278.9 3.0 collective-permute-start.13
  281.9 11.0 %collective-permute-done.5 = bf16[48,1792]{1,0:T(8,128)(2,1)S(1)} collective-permute-done((bf16[48,1792]{1,0:T(8,128)(2,1)S(1)}, bf16[48,1792]{1,0:T(8,128)(2,1)S(1)}, u32[]{:S(2)}, u32[]{:S(2)}) %collective-permute-start.5) | collective-permute-done | bytes 172064 | tf_op jit(solution)/shard_map/ppermute | solution.py:15
  293.0 1.5 convert_element_type.348
  295.3 15.1 %collective-permute-done.13 = bf16[256,1024]{1,0:T(8,128)(2,1)S(1)} collective-permute-done((bf16[256,1024]{1,0:T(8,128)(2,1)}, bf16[256,1024]{1,0:T(8,128)(2,1)S(1)}, u32[]{:S(2)}, u32[]{:S(2)}) %collective-permute-start.13) | collective-permute-done | bytes 524320 | tf_op jit(solution)/shard_map/ppermute | solution.py:15
  310.3 3.1 fusion.8
  313.9 2.6 fusion.38
  316.5 9.0 %all-to-all-start.7 = ((bf16[32,8,1792]{2,1,0:T(8,128)(2,1)}), bf16[32,8,1792]{2,1,0:T(8,128)(2,1)S(1)}, u32[]{:S(2)}, u32[]{:S(2)}) async-start(bf16[32,8,1792]{2,1,0:T(8,128)(2,1)} %bitcast.78), calls=%async_computation.7 | async-start | bytes 1835008 | tf_op jit(solution)/shard_map/all_to_all | solution.py:33
  327.8 23.4 %all-to-all-done.7 = bf16[32,8,1792]{2,1,0:T(8,128)(2,1)S(1)} async-done(((bf16[32,8,1792]{2,1,0:T(8,128)(2,1)}), bf16[32,8,1792]{2,1,0:T(8,128)(2,1)S(1)}, u32[]{:S(2)}, u32[]{:S(2)}) %all-to-all-start.7) | async-done | bytes 917536 | tf_op jit(solution)/shard_map/all_to_all | solution.py:33
  (143 shorter events, 15.8 us)
Async XLA Ops:
  0.6 7.6 %copy-start = (bf16[2,1,48,3584]{3,2,1,0:T(8,128)(2,1)S(1)}, bf16[2,1,48,3584]{3,2,1,0:T(8,128)(2,1)}, u32[]{:S(2)}) copy-start(bf16[2,1,48,3584]{3,2,1,0:T(8,128)(2,1)} %param.11) | copy-start | bytes 2064388
  0.6 11.6 %copy-start.2 = (bf16[1,48,3584]{2,1,0:T(8,128)(2,1)S(1)}, bf16[1,48,3584]{2,1,0:T(8,128)(2,1)}, u32[]{:S(2)}) copy-start(bf16[1,48,3584]{2,1,0:T(8,128)(2,1)} %param.10) | copy-start | bytes 1032196
  0.7 7.9 %copy-start.12 = (f32[4,1,48,2]{2,3,1,0:T(2,128)S(1)}, f32[4,1,48,2]{2,3,1,0:T(2,128)}, u32[]{:S(2)}) copy-start(f32[4,1,48,2]{2,3,1,0:T(2,128)} %param.19) | copy-start | bytes 4612
  0.7 8.5 %copy-start.14 = (s32[4,1,48,2]{2,3,1,0:T(2,128)S(1)}, s32[4,1,48,2]{2,3,1,0:T(2,128)}, u32[]{:S(2)}) copy-start(s32[4,1,48,2]{2,3,1,0:T(2,128)} %param.18) | copy-start | bytes 4612
  0.7 8.5 %copy-start.15 = (s32[4,1,48,2]{2,3,1,0:T(2,128)S(1)}, s32[4,1,48,2]{2,3,1,0:T(2,128)}, u32[]{:S(2)}) copy-start(s32[4,1,48,2]{2,3,1,0:T(2,128)} %param.17) | copy-start | bytes 4612
  0.7 11.8 %copy-start.13 = (f32[1,3584]{1,0:T(1,128)S(1)}, f32[1,3584]{1,0:T(1,128)}, u32[]{:S(2)}) copy-start(f32[1,3584]{1,0:T(1,128)} %param.13) | copy-start | bytes 43012
  3.6 21.6 %collective-permute-start.3 = (bf16[2,48,1792]{2,1,0:T(8,128)(2,1)}, bf16[2,48,1792]{2,1,0:T(8,128)(2,1)S(1)}, u32[]{:S(2)}, u32[]{:S(2)}) collective-permute-start(bf16[2,48,1792]{2,1,0:T(8,128)(2,1)} %fusion.124), channel_id=1, source_target_pairs={{0,1},{1,0},{2,3},{3,2},{4,5},{5,4},{6,7},{7,6},{8,9},{9,8},{10,11... | collective-permute-start | bytes 1032200 | tf_op jit(solution)/shard_map/ppermute | solution.py:15
  8.2 17.0 %copy-start.5 = (bf16[1,48,3584]{2,1,0:T(8,128)(2,1)S(1)}, bf16[1,48,3584]{2,1,0:T(8,128)(2,1)}, u32[]{:S(2)}) copy-start(bf16[1,48,3584]{2,1,0:T(8,128)(2,1)} %param.12) | copy-start | bytes 1032196
  8.2 17.0 %collective-permute-start = (bf16[2,48,1792]{2,1,0:T(8,128)(2,1)}, bf16[2,48,1792]{2,1,0:T(8,128)(2,1)}, u32[]{:S(2)}, u32[]{:S(2)}) collective-permute-start(bf16[2,48,1792]{2,1,0:T(8,128)(2,1)} %fusion.126), channel_id=1, source_target_pairs={{0,1},{1,0},{2,3},{3,2},{4,5},{5,4},{6,7},{7,6},{8,9},{9,8},{10,11... | collective-permute-start | bytes 1032200 | tf_op jit(solution)/shard_map/ppermute | solution.py:15
  9.2 15.1 %collective-permute-start.1 = (f32[18,48]{1,0:T(8,128)S(1)}, f32[18,48]{1,0:T(8,128)S(1)}, u32[]{:S(2)}, u32[]{:S(2)}) collective-permute-start(f32[18,48]{1,0:T(8,128)S(1)} %pad_maximum_fusion.8), channel_id=1, source_target_pairs={{0,1},{1,0},{2,3},{3,2},{4,5},{5,4},{6,7},{7,6},{8,9},{9,8},{10,11... | collective-permute-start | bytes 10376 | tf_op jit(solution)/shard_map/ppermute | solution.py:15
  14.1 35.8 %all-to-all-start = ((bf16[32,8,1792]{2,1,0:T(8,128)(2,1)}), bf16[32,8,1792]{2,1,0:T(8,128)(2,1)S(1)}, u32[]{:S(2)}, u32[]{:S(2)}) async-start(bf16[32,8,1792]{2,1,0:T(8,128)(2,1)} %fusion.50), calls=%async_computation | async-start | bytes 1835008 | tf_op jit(solution)/shard_map/all_to_all | solution.py:33
  50.0 48.9 %all-to-all-start.1 = ((bf16[16,32,1792]{2,1,0:T(8,128)(2,1)}), bf16[16,32,1792]{2,1,0:T(8,128)(2,1)S(1)}, u32[]{:S(2)}, u32[]{:S(2)}) async-start(bf16[16,32,1792]{2,1,0:T(8,128)(2,1)} %pad_maximum_fusion), calls=%async_computation.1 | async-start | bytes 3670016 | tf_op jit(solution)/shard_map/all_to_all | solution.py:33
  55.2 3.3 copy-start.23
  58.5 3.3 copy-start.3
  58.6 3.3 copy-start.4
  58.6 3.3 copy-start.16
  59.7 26.7 %copy-start.18 = (bf16[1,1,1024,1792]{3,2,1,0:T(8,128)(2,1)S(1)}, bf16[1,1,1024,1792]{3,2,1,0:T(8,128)(2,1)}, u32[]{:S(2)}) copy-start(bf16[1,1,1024,1792]{3,2,1,0:T(8,128)(2,1)} %param.16) | copy-start | bytes 11010052
  59.8 26.3 %collective-permute-start.2 = (bf16[256,2048]{1,0:T(8,128)(2,1)S(1)}, bf16[256,2048]{1,0:T(8,128)(2,1)S(1)}, u32[]{:S(2)}, u32[]{:S(2)}) collective-permute-start(bf16[256,2048]{1,0:T(8,128)(2,1)S(1)} %pad_maximum_fusion.3), channel_id=1, source_target_pairs={{0,1},{1,0},{2,3},{3,2},{4,5},{5,4},{6,7},{7,6},{8,9},{9,8},{10,11... | collective-permute-start | bytes 3145736 | tf_op jit(solution)/shard_map/ppermute | solution.py:15
  98.9 2.4 copy-start.20
  101.2 2.3 copy-start.24
  103.5 2.3 copy-start.8
  107.3 4.8 %copy-start.9 = (bf16[16,16,1792]{2,1,0:T(8,128)(2,1)S(1)}, bf16[16,16,1792]{2,1,0:T(8,128)(2,1)}, u32[]{:S(2)}) copy-start(bf16[16,16,1792]{2,1,0:T(8,128)(2,1)} %get-tuple-element.20) | copy-start | bytes 2752516
  107.3 50.9 %all-to-all-start.2 = ((bf16[16,32,1792]{2,1,0:T(8,128)(2,1)}), bf16[16,32,1792]{2,1,0:T(8,128)(2,1)S(1)}, u32[]{:S(2)}, u32[]{:S(2)}) async-start(bf16[16,32,1792]{2,1,0:T(8,128)(2,1)} %pad_maximum_fusion.1), calls=%async_computation.2 | async-start | bytes 3670016 | tf_op jit(solution)/shard_map/all_to_all | solution.py:33
  112.1 3.3 copy-start.10
  112.1 3.3 copy-start.11
  115.5 37.8 %copy-start.21 = (bf16[1,1,1792,1024]{3,2,1,0:T(8,128)(2,1)S(1)}, bf16[1,1,1792,1024]{3,2,1,0:T(8,128)(2,1)}, u32[]{:S(2)}) copy-start(bf16[1,1,1792,1024]{3,2,1,0:T(8,128)(2,1)} %param.15) | copy-start | bytes 11010052
  115.5 37.8 %copy-start.35 = (f32[256,1024]{1,0:T(8,128)S(1)}, f32[256,1024]{1,0:T(8,128)}, u32[]{:S(2)}) copy-start(f32[256,1024]{1,0:T(8,128)} %get-tuple-element.85) | copy-start | bytes 3145732
  115.5 37.5 %collective-permute-start.8 = (bf16[256,3072]{1,0:T(8,128)(2,1)S(1)}, bf16[256,3072]{1,0:T(8,128)(2,1)S(1)}, u32[]{:S(2)}, u32[]{:S(2)}) collective-permute-start(bf16[256,3072]{1,0:T(8,128)(2,1)S(1)} %pad_maximum_fusion.2), channel_id=1, source_target_pairs={{0,1},{1,0},{2,3},{3,2},{4,5},{5,4},{6,7},{7,6},{8,9},{9,8},{10,11... | collective-permute-start | bytes 4718600 | tf_op jit(solution)/shard_map/ppermute | solution.py:15
  153.4 2.0 copy-start.25
  153.4 2.3 copy-start.34
  159.2 33.1 %all-to-all-start.3 = ((bf16[16,16,1792]{2,1,0:T(8,128)(2,1)}), bf16[16,16,1792]{2,1,0:T(8,128)(2,1)S(1)}, u32[]{:S(2)}, u32[]{:S(2)}) async-start(bf16[16,16,1792]{2,1,0:T(8,128)(2,1)} %bitcast.292), calls=%async_computation.3 | async-start | bytes 1835008 | tf_op jit(solution)/shard_map/all_to_all | solution.py:33
  168.9 10.0 %collective-permute-start.6 = (f32[1,96]{1,0:T(1,128)S(1)}, f32[1,96]{1,0:T(1,128)S(1)}, u32[]{:S(2)}, u32[]{:S(2)}) collective-permute-start(f32[1,96]{1,0:T(1,128)S(1)} %bitcast.300), channel_id=1, source_target_pairs={{0,32},{1,33},{32,64},{33,65},{64,96},{65,97},{96,128},{97,129},{1... | collective-permute-start | bytes 1160 | tf_op jit(solution)/shard_map/ppermute | solution.py:27
  171.9 7.0 %collective-permute-start.7 = (f32[1,96]{1,0:T(1,128)S(1)}, f32[1,96]{1,0:T(1,128)S(1)}, u32[]{:S(2)}, u32[]{:S(2)}) collective-permute-start(f32[1,96]{1,0:T(1,128)S(1)} %bitcast.301), channel_id=1, source_target_pairs={{0,33},{1,32},{32,65},{33,64},{64,97},{65,96},{96,129},{97,128},{1... | collective-permute-start | bytes 1160 | tf_op jit(solution)/shard_map/ppermute | solution.py:27
  175.9 11.8 %collective-permute-start.4 = (bf16[96,1792]{1,0:T(8,128)(2,1)S(1)}, bf16[96,1792]{1,0:T(8,128)(2,1)S(1)}, u32[]{:S(2)}, u32[]{:S(2)}) collective-permute-start(bf16[96,1792]{1,0:T(8,128)(2,1)S(1)} %get-tuple-element.79), channel_id=1, source_target_pairs={{0,32},{1,33},{32,64},{33,65},{64,96},{65,97},{96,128},{97,129},{1... | collective-permute-start | bytes 1032200 | tf_op jit(solution)/shard_map/ppermute | solution.py:27
  192.7 30.5 %all-to-all-start.4 = ((bf16[16,16,1792]{2,1,0:T(8,128)(2,1)}), bf16[16,16,1792]{2,1,0:T(8,128)(2,1)}, u32[]{:S(2)}, u32[]{:S(2)}) async-start(bf16[16,16,1792]{2,1,0:T(8,128)(2,1)} %bitcast.57), calls=%async_computation.4 | async-start | bytes 1835008 | tf_op jit(solution)/shard_map/all_to_all | solution.py:33
  197.8 6.8 %copy-start.6 = (bf16[16,16,1792]{2,1,0:T(8,128)(2,1)S(1)}, bf16[16,16,1792]{2,1,0:T(8,128)(2,1)}, u32[]{:S(2)}) copy-start(bf16[16,16,1792]{2,1,0:T(8,128)(2,1)} %get-tuple-element.18) | copy-start | bytes 2752516
  197.8 6.8 %copy-start.26 = (bf16[1,1,1792,1024]{3,2,1,0:T(8,128)(2,1)S(1)}, bf16[1,1,1792,1024]{3,2,1,0:T(8,128)(2,1)}, u32[]{:S(2)}) copy-start(bf16[1,1,1792,1024]{3,2,1,0:T(8,128)(2,1)} %param.14) | copy-start | bytes 11010052
  198.3 4.0 %collective-permute-start.10 = (f32[1,96]{1,0:T(1,128)S(1)}, f32[1,96]{1,0:T(1,128)S(1)}, u32[]{:S(2)}, u32[]{:S(2)}) collective-permute-start(f32[1,96]{1,0:T(1,128)S(1)} %bitcast.302), channel_id=1, source_target_pairs={{0,1},{1,0},{2,3},{3,2},{4,5},{5,4},{6,7},{7,6},{8,9},{9,8},{10,11... | collective-permute-start | bytes 1160 | tf_op jit(solution)/shard_map/ppermute | solution.py:15
  202.5 10.2 %collective-permute-start.11 = (bf16[96,1792]{1,0:T(8,128)(2,1)S(1)}, bf16[96,1792]{1,0:T(8,128)(2,1)S(1)}, u32[]{:S(2)}, u32[]{:S(2)}) collective-permute-start(bf16[96,1792]{1,0:T(8,128)(2,1)S(1)} %fusion.88), channel_id=1, source_target_pairs={{32,0},{33,1},{64,32},{65,33},{96,64},{97,65},{128,96},{129,97},{1... | collective-permute-start | bytes 1032200 | tf_op jit(solution)/shard_map/ppermute | solution.py:27
  223.2 4.7 %copy-start.27 = (bf16[1,1,1792,1024]{3,2,1,0:T(8,128)(2,1)S(1)}, bf16[1,1,1792,1024]{3,2,1,0:T(8,128)(2,1)}, u32[]{:S(2)}) copy-start(bf16[1,1,1792,1024]{3,2,1,0:T(8,128)(2,1)} %param.14) | copy-start | bytes 11010052
  231.4 6.3 %copy-start.7 = (bf16[16,16,1792]{2,1,0:T(8,128)(2,1)S(1)}, bf16[16,16,1792]{2,1,0:T(8,128)(2,1)}, u32[]{:S(2)}) copy-start(bf16[16,16,1792]{2,1,0:T(8,128)(2,1)} %get-tuple-element.18) | copy-start | bytes 2752516
  231.4 34.2 %all-to-all-start.5 = ((bf16[16,16,1792]{2,1,0:T(8,128)(2,1)}), bf16[16,16,1792]{2,1,0:T(8,128)(2,1)S(1)}, u32[]{:S(2)}, u32[]{:S(2)}) async-start(bf16[16,16,1792]{2,1,0:T(8,128)(2,1)} %bitcast.64), calls=%async_computation.5 | async-start | bytes 1835008 | tf_op jit(solution)/shard_map/all_to_all | solution.py:33
  236.4 26.7 %collective-permute-start.9 = (bf16[256,2048]{1,0:T(8,128)(2,1)S(1)}, bf16[256,2048]{1,0:T(8,128)(2,1)S(1)}, u32[]{:S(2)}, u32[]{:S(2)}) collective-permute-start(bf16[256,2048]{1,0:T(8,128)(2,1)S(1)} %pad_maximum_fusion.4), channel_id=1, source_target_pairs={{0,1},{1,0},{2,3},{3,2},{4,5},{5,4},{6,7},{7,6},{8,9},{9,8},{10,11... | collective-permute-start | bytes 3145736 | tf_op jit(solution)/shard_map/ppermute | solution.py:15
  241.8 21.5 %copy-start.19 = (bf16[1,1,1024,1792]{3,2,1,0:T(8,128)(2,1)S(1)}, bf16[1,1,1024,1792]{3,2,1,0:T(8,128)(2,1)}, u32[]{:S(2)}) copy-start(bf16[1,1,1024,1792]{3,2,1,0:T(8,128)(2,1)} %param.16) | copy-start | bytes 11010052
  241.8 21.5 %copy-start.31 = (f32[256,1024]{1,0:T(8,128)S(1)}, f32[256,1024]{1,0:T(8,128)}, u32[]{:S(2)}) copy-start(f32[256,1024]{1,0:T(8,128)} %get-tuple-element.87) | copy-start | bytes 3145732
  241.8 21.5 %copy-start.33 = (f32[256,1024]{1,0:T(8,128)S(1)}, f32[256,1024]{1,0:T(8,128)}, u32[]{:S(2)}) copy-start(f32[256,1024]{1,0:T(8,128)} %get-tuple-element.89) | copy-start | bytes 3145732
  242.9 50.0 %collective-permute-start.14 = (bf16[256,2048]{1,0:T(8,128)(2,1)}, bf16[256,2048]{1,0:T(8,128)(2,1)}, u32[]{:S(2)}, u32[]{:S(2)}) collective-permute-start(bf16[256,2048]{1,0:T(8,128)(2,1)} %pad_maximum_fusion.5), channel_id=1, source_target_pairs={{0,1},{1,0},{2,3},{3,2},{4,5},{5,4},{6,7},{7,6},{8,9},{9,8},{10,11... | collective-permute-start | bytes 3145736 | tf_op jit(solution)/shard_map/ppermute | solution.py:15
  244.9 48.0 %collective-permute-start.5 = (bf16[48,1792]{1,0:T(8,128)(2,1)S(1)}, bf16[48,1792]{1,0:T(8,128)(2,1)S(1)}, u32[]{:S(2)}, u32[]{:S(2)}) collective-permute-start(bf16[48,1792]{1,0:T(8,128)(2,1)S(1)} %broadcast_select_fusion.6), channel_id=1, source_target_pairs={{0,1},{1,0},{2,3},{3,2},{4,5},{5,4},{6,7},{7,6},{8,9},{9,8},{10,11... | collective-permute-start | bytes 516104 | tf_op jit(solution)/shard_map/ppermute | solution.py:15
  269.9 46.5 %all-to-all-start.6 = ((bf16[32,8,1792]{2,1,0:T(8,128)(2,1)}), bf16[32,8,1792]{2,1,0:T(8,128)(2,1)S(1)}, u32[]{:S(2)}, u32[]{:S(2)}) async-start(bf16[32,8,1792]{2,1,0:T(8,128)(2,1)} %bitcast.66), calls=%async_computation.6 | async-start | bytes 1835008 | tf_op jit(solution)/shard_map/all_to_all | solution.py:33
  278.9 31.4 %copy-start.22 = (bf16[1,1,1792,1024]{3,2,1,0:T(8,128)(2,1)S(1)}, bf16[1,1,1792,1024]{3,2,1,0:T(8,128)(2,1)}, u32[]{:S(2)}) copy-start(bf16[1,1,1792,1024]{3,2,1,0:T(8,128)(2,1)} %param.15) | copy-start | bytes 11010052
  278.9 31.4 %collective-permute-start.13 = (bf16[256,1024]{1,0:T(8,128)(2,1)}, bf16[256,1024]{1,0:T(8,128)(2,1)S(1)}, u32[]{:S(2)}, u32[]{:S(2)}) collective-permute-start(bf16[256,1024]{1,0:T(8,128)(2,1)} %get-tuple-element.92), channel_id=1, source_target_pairs={{0,1},{1,0},{2,3},{3,2},{4,5},{5,4},{6,7},{7,6},{8,9},{9,8},{10,11... | collective-permute-start | bytes 1572872 | tf_op jit(solution)/shard_map/ppermute | solution.py:15
  294.5 31.0 %collective-permute-start.12 = (bf16[48,1792]{1,0:T(8,128)(2,1)S(1)}, bf16[48,1792]{1,0:T(8,128)(2,1)S(1)}, u32[]{:S(2)}, u32[]{:S(2)}) collective-permute-start(bf16[48,1792]{1,0:T(8,128)(2,1)S(1)} %broadcast_select_fusion.4), channel_id=1, source_target_pairs={{0,1},{1,0},{2,3},{3,2},{4,5},{5,4},{6,7},{7,6},{8,9},{9,8},{10,11... | collective-permute-start | bytes 516104 | tf_op jit(solution)/shard_map/ppermute | solution.py:15
  310.3 3.1 copy-start.28
  310.3 3.1 copy-start.29
  310.3 3.3 copy-start.30
  310.3 3.6 %copy-start.32 = (f32[256,1024]{1,0:T(8,128)S(1)}, f32[256,1024]{1,0:T(8,128)}, u32[]{:S(2)}) copy-start(f32[256,1024]{1,0:T(8,128)} %get-tuple-element.93) | copy-start | bytes 3145732
  316.5 34.7 %all-to-all-start.7 = ((bf16[32,8,1792]{2,1,0:T(8,128)(2,1)}), bf16[32,8,1792]{2,1,0:T(8,128)(2,1)S(1)}, u32[]{:S(2)}, u32[]{:S(2)}) async-start(bf16[32,8,1792]{2,1,0:T(8,128)(2,1)} %bitcast.78), calls=%async_computation.7 | async-start | bytes 1835008 | tf_op jit(solution)/shard_map/all_to_all | solution.py:33
  326.8 25.6 %copy-start.1 = (bf16[2,1,48,3584]{3,2,1,0:T(8,128)(2,1)S(1)}, bf16[2,1,48,3584]{3,2,1,0:T(8,128)(2,1)}, u32[]{:S(2)}) copy-start(bf16[2,1,48,3584]{3,2,1,0:T(8,128)(2,1)} %param.11) | copy-start | bytes 2064388
  351.1 1.6 copy-start.17
